TPU v7x, 512 devices: a whole 4x8x8 slice. The times are simulated.
512 devices in a mesh: pre: 64 (over z, x, core), head: 8 (over y).
Axes of the slice: x: 4, y: 8, z: 8, core: 2. Of those that a mesh axis runs over, the one named last changes fastest.
Arguments:
- queries: bfloat16 [2048, 64, 3, 128], P('pre', 'head'), may hold values from -8 to 8
- prefix_keys: bfloat16 [64, 512, 8, 128], P('pre', None, 'head'), may hold values from -8 to 8
- prefix_values: bfloat16 [64, 512, 8, 128], P('pre', None, 'head'), may hold values from -4 to 4
- suffix_keys: bfloat16 [2048, 96, 8, 128], P('pre', None, 'head'), may hold values from -8 to 8
- suffix_values: bfloat16 [2048, 96, 8, 128], P('pre', None, 'head'), may hold values from -4 to 4
- new_keys: bfloat16 [2048, 3, 8, 128], P('pre', None, 'head'), may hold values from -8 to 8
- new_values: bfloat16 [2048, 3, 8, 128], P('pre', None, 'head'), may hold values from -4 to 4
- suffix_lengths: int32 [2048], P('pre'), may hold values from 48 to 96, as said below
- prefix_of_row: int32 [2048], P('pre'), may hold values from 0 to 63, as said below
- owner_of_prefix: int32 [64], replicated, may hold values from 0 to 63, each once
Outputs:
- attended: bfloat16 [2048, 64, 3, 128], P(('pre', 'head'))
Inputs may be any that keep to these rules, and one draw needn't show every extreme that they name: `suffix_lengths`: every device's rows include at least one of length 96. `prefix_of_row`: the rows of one device name exactly 16 different prefixes, each by exactly 2 rows; one prefix is named on every device.
All inputs are finite; a program needn't handle non-finite values.
Results may differ from a plain program's by a relative error of at most 0.0027.
Values may be sent and summed in bfloat16 or wider, within the bound.
A program may use at most 64 MiB of HBM per device.

v0:
```python
import jax
import jax.numpy as jnp
from jax import lax
from jax.sharding import PartitionSpec as P

masked_score = -1e30


def shards(
    queries,
    prefix_keys,
    prefix_values,
    suffix_keys,
    suffix_values,
    new_keys,
    new_values,
    suffix_lengths,
    prefix_of_row,
    owner_of_prefix,
):
    row_count, head_count, step_count, head_width = queries.shape
    kv_heads = suffix_keys.shape[2]
    group_size = head_count // kv_heads
    suffix_span = suffix_keys.shape[1]
    owner_count = lax.axis_size("pre")
    per_prompt = max(2, row_count // owner_count)
    score_scale = head_width ** (-0.5)
    prefix_count = owner_of_prefix.shape[0]
    row_index = jnp.arange(row_count, dtype=jnp.int32)
    lookup = prefix_of_row[:, None] == jnp.arange(prefix_count, dtype=jnp.int32)[None, :]
    owner_row = jnp.sum(jnp.where(lookup, owner_of_prefix[None, :], 0), axis=1)
    earlier = (owner_row[:, None] == owner_row[None, :]) & (row_index[None, :] < row_index[:, None])
    row_rank = jnp.sum(earlier.astype(jnp.int32), axis=1)
    slot_row = owner_row * per_prompt + row_rank
    slot_match = slot_row[None, :] == jnp.arange(owner_count * per_prompt, dtype=jnp.int32)[:, None]
    source = jnp.sum(jnp.where(slot_match, row_index[None, :], 0), axis=1)
    filled = jnp.any(slot_match, axis=1)
    grouped = queries.reshape(row_count, kv_heads, group_size, step_count, head_width)
    outgoing = jnp.where(
        filled[:, None, None, None, None],
        jnp.take(grouped, source, axis=0),
        jnp.zeros((), jnp.bfloat16),
    )
    keys_here = prefix_keys[0]
    values_here = prefix_values[0]
    returned = []
    for step_index in range(step_count):
        received = lax.all_to_all(
            outgoing[:, :, :, step_index : step_index + 1],
            "pre",
            split_axis=0,
            concat_axis=0,
            tiled=True,
        )
        slot_total, unused, item_count, span_steps, unused_width = received.shape
        flattened = received[:, 0].reshape(slot_total * item_count * span_steps, head_width)
        block_rows = flattened.shape[0]
        while block_rows > 1024 and block_rows % 2 == 0:
            block_rows = block_rows // 2
        prefix_key = keys_here[:, 0]
        prefix_value = values_here[:, 0]

        def score_block(query_block):
            scores = (
                lax.dot_general(
                    query_block,
                    prefix_key,
                    (((1,), (1,)), ((), ())),
                    preferred_element_type=jnp.float32,
                )
                * score_scale
            )
            row_max = jnp.max(scores, axis=1)
            expo = jnp.exp(scores - row_max[:, None])
            row_sum = jnp.sum(expo, axis=1)
            weighted = jnp.dot(
                expo.astype(jnp.bfloat16), prefix_value, preferred_element_type=jnp.float32
            )
            return (weighted, row_max, row_sum)

        weighted, row_max, row_sum = lax.map(
            score_block, flattened.reshape(-1, block_rows, head_width)
        )
        weighted_list = [weighted.reshape(slot_total, item_count, span_steps, head_width)]
        max_list = [row_max.reshape(slot_total, item_count, span_steps)]
        sum_list = [row_sum.reshape(slot_total, item_count, span_steps)]
        owner_part = jnp.stack(weighted_list, axis=1)
        owner_max = jnp.stack(max_list, axis=1)
        owner_sum = jnp.stack(sum_list, axis=1)
        returned.append(
            (
                lax.all_to_all(owner_part, "pre", split_axis=0, concat_axis=0, tiled=True),
                lax.all_to_all(owner_max, "pre", split_axis=0, concat_axis=0, tiled=True),
                lax.all_to_all(owner_sum, "pre", split_axis=0, concat_axis=0, tiled=True),
            )
        )
    back_part = jnp.concatenate([piece[0] for piece in returned], axis=3)
    back_max = jnp.concatenate([piece[1] for piece in returned], axis=3)
    back_sum = jnp.concatenate([piece[2] for piece in returned], axis=3)
    pre_part = jnp.take(back_part, slot_row, axis=0)
    pre_max = jnp.take(back_max, slot_row, axis=0)
    pre_sum = jnp.take(back_sum, slot_row, axis=0)
    suffix_scores = (
        jnp.einsum("rkgtd,rskd->rkgts", grouped, suffix_keys, preferred_element_type=jnp.float32)
        * score_scale
    )
    fresh_scores = (
        jnp.einsum("rkgtd,rukd->rkgtu", grouped, new_keys, preferred_element_type=jnp.float32)
        * score_scale
    )
    in_range = (jnp.arange(suffix_span, dtype=jnp.int32)[None, :] < suffix_lengths[:, None])[
        :, None, None, None, :
    ]
    step_ids = jnp.arange(step_count, dtype=jnp.int32)
    causal = (step_ids[None, :] <= step_ids[:, None])[None, None, None, :, :]
    suffix_scores = jnp.where(in_range, suffix_scores, masked_score)
    fresh_scores = jnp.where(causal, fresh_scores, masked_score)
    local_max = jnp.maximum(jnp.max(suffix_scores, axis=-1), jnp.max(fresh_scores, axis=-1))
    suffix_exp = jnp.where(in_range, jnp.exp(suffix_scores - local_max[..., None]), 0.0)
    fresh_exp = jnp.where(causal, jnp.exp(fresh_scores - local_max[..., None]), 0.0)
    local_sum = jnp.sum(suffix_exp, axis=-1) + jnp.sum(fresh_exp, axis=-1)
    local_part = jnp.einsum(
        "rkgts,rskd->rkgtd",
        suffix_exp.astype(jnp.bfloat16),
        suffix_values,
        preferred_element_type=jnp.float32,
    )
    local_part = local_part + jnp.einsum(
        "rkgtu,rukd->rkgtd",
        fresh_exp.astype(jnp.bfloat16),
        new_values,
        preferred_element_type=jnp.float32,
    )
    combined_max = jnp.maximum(pre_max, local_max)
    pre_factor = jnp.exp(pre_max - combined_max)
    local_factor = jnp.exp(local_max - combined_max)
    attended = (pre_part * pre_factor[..., None] + local_part * local_factor[..., None]) / (
        pre_sum * pre_factor + local_sum * local_factor
    )[..., None]
    attended = attended.astype(jnp.bfloat16).reshape(row_count, head_count, step_count, head_width)
    return lax.all_to_all(attended, "head", split_axis=0, concat_axis=1, tiled=True)


def solution(mesh):
    in_specs = (
        P("pre", "head", None, None),
        P("pre", None, "head", None),
        P("pre", None, "head", None),
        P("pre", None, "head", None),
        P("pre", None, "head", None),
        P("pre", None, "head", None),
        P("pre", None, "head", None),
        P("pre"),
        P("pre"),
        P(),
    )
    out_specs = P(("pre", "head"), None, None, None)
    return jax.shard_map(shards, mesh=mesh, in_specs=in_specs, out_specs=out_specs, check_vma=False)
```

profile of v0, /device:TPU:1, one launch (start us, length us, event | category | flops | bytes accessed | tf_op | source)
XLA Modules:
  0.0 245.9 jit_solution(16735387866116440248)
XLA Ops:
  1.3 1.7 gather_fusion
  4.2 27.8 %all_to_all.78 = bf16[128,1,8,1,128]{4,2,3,1,0:T(8,128)(2,1)S(1)} all-to-all(bf16[128,1,8,1,128]{4,2,3,1,0:T(8,128)(2,1)S(1)} %get-tuple-element.70), channel_id=1, replica_groups=mesh['pre'=64,'head'=8] {'pre'}, dimensions={0} | all-to-all | bytes 524288 | tf_op jit(solution)/shard_map/all_to_all | solution.py:48
  32.0 17.7 %all_to_all.79 = bf16[128,1,8,1,128]{4,2,3,1,0:T(8,128)(2,1)S(1)} all-to-all(bf16[128,1,8,1,128]{4,2,3,1,0:T(8,128)(2,1)S(1)} %get-tuple-element.72), channel_id=1, replica_groups=mesh['pre'=64,'head'=8] {'pre'}, dimensions={0} | all-to-all | bytes 524288 | tf_op jit(solution)/shard_map/all_to_all | solution.py:48
  49.7 4.7 %all-to-all-start.4 = ((bf16[128,1,8,1,128]{4,2,3,1,0:T(8,128)(2,1)}), bf16[128,1,8,1,128]{4,2,3,1,0:T(8,128)(2,1)S(1)}, u32[]{:S(2)}, u32[]{:S(2)}) async-start(bf16[128,1,8,1,128]{4,2,3,1,0:T(8,128)(2,1)} %get-tuple-element.71), calls=%async_computation.4 | async-start | bytes 524288 | tf_op jit(solution)/shard_map/all_to_all | solution.py:48
  54.9 1.4 fusion.2
  57.1 10.5 %all-to-all-done.4 = bf16[128,1,8,1,128]{4,2,3,1,0:T(8,128)(2,1)S(1)} async-done(((bf16[128,1,8,1,128]{4,2,3,1,0:T(8,128)(2,1)}), bf16[128,1,8,1,128]{4,2,3,1,0:T(8,128)(2,1)S(1)}, u32[]{:S(2)}, u32[]{:S(2)}) %all-to-all-start.4) | async-done | bytes 262176 | tf_op jit(solution)/shard_map/all_to_all | solution.py:48
  67.6 5.0 %all-to-all-start.10 = ((f32[128,1,8,1]{2,3,1,0:T(1,128)}), f32[128,1,8,1]{2,3,1,0:T(1,128)}, u32[]{:S(2)}, u32[]{:S(2)}) async-start(f32[128,1,8,1]{2,3,1,0:T(1,128)} %bitcast.45), calls=%async_computation.10 | async-start | bytes 131072 | tf_op jit(solution)/shard_map/all_to_all | solution.py:94
  73.9 8.8 %all-to-all-done.10 = f32[128,1,8,1]{2,3,1,0:T(1,128)} async-done(((f32[128,1,8,1]{2,3,1,0:T(1,128)}), f32[128,1,8,1]{2,3,1,0:T(1,128)}, u32[]{:S(2)}, u32[]{:S(2)}) %all-to-all-start.10) | async-done | bytes 4128 | tf_op jit(solution)/shard_map/all_to_all | solution.py:94
  82.7 4.4 %all-to-all-start.7 = ((f32[128,1,8,1]{2,3,1,0:T(1,128)}), f32[128,1,8,1]{2,3,1,0:T(1,128)S(1)}, u32[]{:S(2)}, u32[]{:S(2)}) async-start(f32[128,1,8,1]{2,3,1,0:T(1,128)} %bitcast.24), calls=%async_computation.7 | async-start | bytes 131072 | tf_op jit(solution)/shard_map/all_to_all | solution.py:93
  87.1 1.4 fusion.4
  89.3 8.0 %all-to-all-done.7 = f32[128,1,8,1]{2,3,1,0:T(1,128)S(1)} async-done(((f32[128,1,8,1]{2,3,1,0:T(1,128)}), f32[128,1,8,1]{2,3,1,0:T(1,128)S(1)}, u32[]{:S(2)}, u32[]{:S(2)}) %all-to-all-start.7) | async-done | bytes 4128 | tf_op jit(solution)/shard_map/all_to_all | solution.py:93
  97.3 4.4 %all-to-all-start.11 = ((f32[128,1,8,1]{2,3,1,0:T(1,128)}), f32[128,1,8,1]{2,3,1,0:T(1,128)S(1)}, u32[]{:S(2)}, u32[]{:S(2)}) async-start(f32[128,1,8,1]{2,3,1,0:T(1,128)} %bitcast.47), calls=%async_computation.11 | async-start | bytes 131072 | tf_op jit(solution)/shard_map/all_to_all | solution.py:94
  102.9 8.9 %all-to-all-done.11 = f32[128,1,8,1]{2,3,1,0:T(1,128)S(1)} async-done(((f32[128,1,8,1]{2,3,1,0:T(1,128)}), f32[128,1,8,1]{2,3,1,0:T(1,128)S(1)}, u32[]{:S(2)}, u32[]{:S(2)}) %all-to-all-start.11) | async-done | bytes 4128 | tf_op jit(solution)/shard_map/all_to_all | solution.py:94
  111.8 4.4 %all-to-all-start.8 = ((f32[128,1,8,1]{2,3,1,0:T(1,128)}), f32[128,1,8,1]{2,3,1,0:T(1,128)S(1)}, u32[]{:S(2)}, u32[]{:S(2)}) async-start(f32[128,1,8,1]{2,3,1,0:T(1,128)} %bitcast.26), calls=%async_computation.8 | async-start | bytes 131072 | tf_op jit(solution)/shard_map/all_to_all | solution.py:93
  116.3 1.4 fusion
  118.4 8.0 %all-to-all-done.8 = f32[128,1,8,1]{2,3,1,0:T(1,128)S(1)} async-done(((f32[128,1,8,1]{2,3,1,0:T(1,128)}), f32[128,1,8,1]{2,3,1,0:T(1,128)S(1)}, u32[]{:S(2)}, u32[]{:S(2)}) %all-to-all-start.8) | async-done | bytes 4128 | tf_op jit(solution)/shard_map/all_to_all | solution.py:93
  126.4 4.4 %all-to-all-start.9 = ((f32[128,1,8,1]{2,3,1,0:T(1,128)}), f32[128,1,8,1]{2,3,1,0:T(1,128)S(1)}, u32[]{:S(2)}, u32[]{:S(2)}) async-start(f32[128,1,8,1]{2,3,1,0:T(1,128)} %bitcast.43), calls=%async_computation.9 | async-start | bytes 131072 | tf_op jit(solution)/shard_map/all_to_all | solution.py:94
  131.6 9.4 %all-to-all-done.9 = f32[128,1,8,1]{2,3,1,0:T(1,128)S(1)} async-done(((f32[128,1,8,1]{2,3,1,0:T(1,128)}), f32[128,1,8,1]{2,3,1,0:T(1,128)S(1)}, u32[]{:S(2)}, u32[]{:S(2)}) %all-to-all-start.9) | async-done | bytes 4128 | tf_op jit(solution)/shard_map/all_to_all | solution.py:94
  141.0 4.6 %all-to-all-start.6 = ((f32[128,1,8,1]{2,3,1,0:T(1,128)}), f32[128,1,8,1]{2,3,1,0:T(1,128)S(1)}, u32[]{:S(2)}, u32[]{:S(2)}) async-start(f32[128,1,8,1]{2,3,1,0:T(1,128)} %bitcast.22), calls=%async_computation.6 | async-start | bytes 131072 | tf_op jit(solution)/shard_map/all_to_all | solution.py:93
  145.6 1.9 convolution_bitcast_fusion.1
  148.7 7.1 %all-to-all-done.6 = f32[128,1,8,1]{2,3,1,0:T(1,128)S(1)} async-done(((f32[128,1,8,1]{2,3,1,0:T(1,128)}), f32[128,1,8,1]{2,3,1,0:T(1,128)S(1)}, u32[]{:S(2)}, u32[]{:S(2)}) %all-to-all-start.6) | async-done | bytes 4128 | tf_op jit(solution)/shard_map/all_to_all | solution.py:93
  156.4 4.5 %all-to-all-start.3 = ((f32[128,1,8,1,128]{4,2,3,1,0:T(8,128)}), f32[128,1,8,1,128]{4,2,3,1,0:T(8,128)S(1)}, u32[]{:S(2)}, u32[]{:S(2)}) async-start(f32[128,1,8,1,128]{4,2,3,1,0:T(8,128)} %copy.63), calls=%async_computation.3 | async-start | bytes 1048576 | tf_op jit(solution)/shard_map/all_to_all | solution.py:92
  162.9 15.8 %all-to-all-done.3 = f32[128,1,8,1,128]{4,2,3,1,0:T(8,128)S(1)} async-done(((f32[128,1,8,1,128]{4,2,3,1,0:T(8,128)}), f32[128,1,8,1,128]{4,2,3,1,0:T(8,128)S(1)}, u32[]{:S(2)}, u32[]{:S(2)}) %all-to-all-start.3) | async-done | bytes 524320 | tf_op jit(solution)/shard_map/all_to_all | solution.py:92
  178.7 5.7 %all-to-all-start.5 = ((f32[128,1,8,1,128]{4,2,3,1,0:T(8,128)}), f32[128,1,8,1,128]{4,2,3,1,0:T(8,128)S(1)}, u32[]{:S(2)}, u32[]{:S(2)}) async-start(f32[128,1,8,1,128]{4,2,3,1,0:T(8,128)} %copy.65), calls=%async_computation.5 | async-start | bytes 1048576 | tf_op jit(solution)/shard_map/all_to_all | solution.py:92
  184.9 2.0 fusion.63
  187.0 2.5 %fusion.62 = (f32[32,8,3]{1,2,0:T(4,128)S(1)}, f32[32,8,3,96]{3,1,2,0:T(8,128)}) fusion(bf16[32,8,3,128]{3,1,2,0:T(8,128)(2,1)S(1)} %copy-done.1, bf16[32,96,1,128]{3,1,2,0:T(8,128)(2,1)} %param.15, pred[32,96]{1,0:T(8,128)(4,1)S(1)} %iota_compare_fusion), kind=kOutput, calls=%fused_computation.106 | convolution fusion | flops 19094784 | bytes 1284096 | tf_op jit(solution)/shard_map/rkgtd,rskd->rkgts/dot_general | solution.py:104
  193.9 8.3 %all-to-all-done.5 = f32[128,1,8,1,128]{4,2,3,1,0:T(8,128)S(1)} async-done(((f32[128,1,8,1,128]{4,2,3,1,0:T(8,128)}), f32[128,1,8,1,128]{4,2,3,1,0:T(8,128)S(1)}, u32[]{:S(2)}, u32[]{:S(2)}) %all-to-all-start.5) | async-done | bytes 524320 | tf_op jit(solution)/shard_map/all_to_all | solution.py:92
  202.1 5.9 %all-to-all-start.1 = ((f32[128,1,8,1,128]{4,2,3,1,0:T(8,128)}), f32[128,1,8,1,128]{4,2,3,1,0:T(8,128)}, u32[]{:S(2)}, u32[]{:S(2)}) async-start(f32[128,1,8,1,128]{4,2,3,1,0:T(8,128)} %copy.61), calls=%async_computation.1 | async-start | bytes 1048576 | tf_op jit(solution)/shard_map/all_to_all | solution.py:92
  209.6 1.1 fusion.18
  210.7 14.9 %all-to-all-done.1 = f32[128,1,8,1,128]{4,2,3,1,0:T(8,128)} async-done(((f32[128,1,8,1,128]{4,2,3,1,0:T(8,128)}), f32[128,1,8,1,128]{4,2,3,1,0:T(8,128)}, u32[]{:S(2)}, u32[]{:S(2)}) %all-to-all-start.1) | async-done | bytes 524320 | tf_op jit(solution)/shard_map/all_to_all | solution.py:92
  227.4 1.7 fusion.10
  229.2 16.0 %all_to_all.80 = bf16[32,8,3,128]{3,1,2,0:T(8,128)(2,1)S(1)} all-to-all(bf16[32,8,3,128]{3,1,2,0:T(8,128)(2,1)S(1)} %fusion.10), channel_id=1, replica_groups=mesh['pre'=64,'head'=8] {'head'}, dimensions={0} | all-to-all | bytes 393216 | tf_op jit(solution)/shard_map/all_to_all | solution.py:141
  (89 shorter events, 20.8 us)
Async XLA Ops:
  0.0 209.6 %copy-start = (bf16[32,96,1,128]{3,1,2,0:T(8,128)(2,1)S(1)}, bf16[32,96,1,128]{3,1,2,0:T(8,128)(2,1)}, u32[]{:S(2)}) copy-start(bf16[32,96,1,128]{3,1,2,0:T(8,128)(2,1)} %param.16) | copy-start | bytes 2359300
  1.1 3.1 %copy-start.21 = (s32[32]{0:T(128)}, s32[32]{0:T(128)S(1)}, u32[]{:S(2)}) copy-start(s32[32]{0:T(128)S(1)} %get-tuple-element.56) | copy-start | bytes 388
  3.0 51.4 %copy-start.5 = (bf16[1,512,1,128]{3,1,2,0:T(8,128)(2,1)S(1)}, bf16[1,512,1,128]{3,1,2,0:T(8,128)(2,1)}, u32[]{:S(2)}) copy-start(bf16[1,512,1,128]{3,1,2,0:T(8,128)(2,1)} %param.13) | copy-start | bytes 393220
  49.7 17.9 %all-to-all-start.4 = ((bf16[128,1,8,1,128]{4,2,3,1,0:T(8,128)(2,1)}), bf16[128,1,8,1,128]{4,2,3,1,0:T(8,128)(2,1)S(1)}, u32[]{:S(2)}, u32[]{:S(2)}) async-start(bf16[128,1,8,1,128]{4,2,3,1,0:T(8,128)(2,1)} %get-tuple-element.71), calls=%async_computation.4 | async-start | bytes 524288 | tf_op jit(solution)/shard_map/all_to_all | solution.py:48
  67.6 15.1 %all-to-all-start.10 = ((f32[128,1,8,1]{2,3,1,0:T(1,128)}), f32[128,1,8,1]{2,3,1,0:T(1,128)}, u32[]{:S(2)}, u32[]{:S(2)}) async-start(f32[128,1,8,1]{2,3,1,0:T(1,128)} %bitcast.45), calls=%async_computation.10 | async-start | bytes 131072 | tf_op jit(solution)/shard_map/all_to_all | solution.py:94
  82.7 14.6 %all-to-all-start.7 = ((f32[128,1,8,1]{2,3,1,0:T(1,128)}), f32[128,1,8,1]{2,3,1,0:T(1,128)S(1)}, u32[]{:S(2)}, u32[]{:S(2)}) async-start(f32[128,1,8,1]{2,3,1,0:T(1,128)} %bitcast.24), calls=%async_computation.7 | async-start | bytes 131072 | tf_op jit(solution)/shard_map/all_to_all | solution.py:93
  97.3 20.5 %copy-start.7 = (f32[128,1,8,1]{2,3,1,0:T(1,128)}, f32[128,1,8,1]{2,3,1,0:T(1,128)S(1)}, u32[]{:S(2)}) copy-start(f32[128,1,8,1]{2,3,1,0:T(1,128)S(1)} %all-to-all-done.7) | copy-start | bytes 12292
  97.3 14.6 %all-to-all-start.11 = ((f32[128,1,8,1]{2,3,1,0:T(1,128)}), f32[128,1,8,1]{2,3,1,0:T(1,128)S(1)}, u32[]{:S(2)}, u32[]{:S(2)}) async-start(f32[128,1,8,1]{2,3,1,0:T(1,128)} %bitcast.47), calls=%async_computation.11 | async-start | bytes 131072 | tf_op jit(solution)/shard_map/all_to_all | solution.py:94
  102.2 43.4 %copy-start.6 = (bf16[1,512,1,128]{3,1,2,0:T(8,128)(2,1)S(1)}, bf16[1,512,1,128]{3,1,2,0:T(8,128)(2,1)}, u32[]{:S(2)}) copy-start(bf16[1,512,1,128]{3,1,2,0:T(8,128)(2,1)} %param.14) | copy-start | bytes 393220
  111.8 35.7 %copy-start.9 = (f32[128,1,8,1]{2,3,1,0:T(1,128)}, f32[128,1,8,1]{2,3,1,0:T(1,128)S(1)}, u32[]{:S(2)}) copy-start(f32[128,1,8,1]{2,3,1,0:T(1,128)S(1)} %all-to-all-done.11) | copy-start | bytes 12292
  111.8 14.6 %all-to-all-start.8 = ((f32[128,1,8,1]{2,3,1,0:T(1,128)}), f32[128,1,8,1]{2,3,1,0:T(1,128)S(1)}, u32[]{:S(2)}, u32[]{:S(2)}) async-start(f32[128,1,8,1]{2,3,1,0:T(1,128)} %bitcast.26), calls=%async_computation.8 | async-start | bytes 131072 | tf_op jit(solution)/shard_map/all_to_all | solution.py:93
  117.7 43.1 %copy-start.22 = (s32[32]{0:T(128)S(1)}, s32[32]{0:T(128)}, u32[]{:S(2)}) copy-start(s32[32]{0:T(128)} %copy-done.21) | copy-start | bytes 388
  117.7 43.2 %copy-start.20 = (s32[32]{0:T(128)S(1)}, s32[32]{0:T(128)}, u32[]{:S(2)}) copy-start(s32[32]{0:T(128)} %param.19) | copy-start | bytes 388
  117.7 43.3 %copy-start.2 = (bf16[128,8,512]{2,1,0:T(8,128)(2,1)S(1)}, bf16[128,8,512]{2,1,0:T(8,128)(2,1)}, u32[]{:S(2)}) copy-start(bf16[128,8,512]{2,1,0:T(8,128)(2,1)} %get-tuple-element.62) | copy-start | bytes 3145732
  126.4 35.3 %copy-start.11 = (f32[128,1,8,1]{2,3,1,0:T(1,128)}, f32[128,1,8,1]{2,3,1,0:T(1,128)S(1)}, u32[]{:S(2)}) copy-start(f32[128,1,8,1]{2,3,1,0:T(1,128)S(1)} %all-to-all-done.8) | copy-start | bytes 12292
  126.4 14.6 %all-to-all-start.9 = ((f32[128,1,8,1]{2,3,1,0:T(1,128)}), f32[128,1,8,1]{2,3,1,0:T(1,128)S(1)}, u32[]{:S(2)}, u32[]{:S(2)}) async-start(f32[128,1,8,1]{2,3,1,0:T(1,128)} %bitcast.43), calls=%async_computation.9 | async-start | bytes 131072 | tf_op jit(solution)/shard_map/all_to_all | solution.py:94
  141.0 14.8 %all-to-all-start.6 = ((f32[128,1,8,1]{2,3,1,0:T(1,128)}), f32[128,1,8,1]{2,3,1,0:T(1,128)S(1)}, u32[]{:S(2)}, u32[]{:S(2)}) async-start(f32[128,1,8,1]{2,3,1,0:T(1,128)} %bitcast.22), calls=%async_computation.6 | async-start | bytes 131072 | tf_op jit(solution)/shard_map/all_to_all | solution.py:93
  156.4 22.3 %all-to-all-start.3 = ((f32[128,1,8,1,128]{4,2,3,1,0:T(8,128)}), f32[128,1,8,1,128]{4,2,3,1,0:T(8,128)S(1)}, u32[]{:S(2)}, u32[]{:S(2)}) async-start(f32[128,1,8,1,128]{4,2,3,1,0:T(8,128)} %copy.63), calls=%async_computation.3 | async-start | bytes 1048576 | tf_op jit(solution)/shard_map/all_to_all | solution.py:92
  160.9 24.1 %copy-start.1 = (bf16[32,8,3,128]{3,1,2,0:T(8,128)(2,1)S(1)}, bf16[32,8,3,128]{3,1,2,0:T(8,128)(2,1)}, u32[]{:S(2)}) copy-start(bf16[32,8,3,128]{3,1,2,0:T(8,128)(2,1)} %param.12) | copy-start | bytes 589828
  160.9 24.1 %copy-start.23 = (bf16[32,3,1,128]{3,0,2,1:T(8,128)(2,1)S(1)}, bf16[32,3,1,128]{3,0,2,1:T(8,128)(2,1)}, u32[]{:S(2)}) copy-start(bf16[32,3,1,128]{3,0,2,1:T(8,128)(2,1)} %param.17) | copy-start | bytes 73732
  161.7 27.7 %copy-start.3 = (bf16[128,8,512]{2,1,0:T(8,128)(2,1)S(1)}, bf16[128,8,512]{2,1,0:T(8,128)(2,1)}, u32[]{:S(2)}) copy-start(bf16[128,8,512]{2,1,0:T(8,128)(2,1)} %get-tuple-element.58) | copy-start | bytes 3145732
  178.7 23.4 %all-to-all-start.5 = ((f32[128,1,8,1,128]{4,2,3,1,0:T(8,128)}), f32[128,1,8,1,128]{4,2,3,1,0:T(8,128)S(1)}, u32[]{:S(2)}, u32[]{:S(2)}) async-start(f32[128,1,8,1,128]{4,2,3,1,0:T(8,128)} %copy.65), calls=%async_computation.5 | async-start | bytes 1048576 | tf_op jit(solution)/shard_map/all_to_all | solution.py:92
  187.0 4.4 %copy-start.8 = (f32[128,1,8,1]{2,3,1,0:T(1,128)S(1)}, f32[128,1,8,1]{2,3,1,0:T(1,128)}, u32[]{:S(2)}) copy-start(f32[128,1,8,1]{2,3,1,0:T(1,128)} %copy-done.7) | copy-start | bytes 12292
  187.0 4.4 %copy-start.12 = (f32[128,1,8,1]{2,3,1,0:T(1,128)S(1)}, f32[128,1,8,1]{2,3,1,0:T(1,128)}, u32[]{:S(2)}) copy-start(f32[128,1,8,1]{2,3,1,0:T(1,128)} %copy-done.11) | copy-start | bytes 12292
  187.0 4.4 %copy-start.14 = (f32[128,1,8,1]{2,3,1,0:T(1,128)S(1)}, f32[128,1,8,1]{2,3,1,0:T(1,128)}, u32[]{:S(2)}) copy-start(f32[128,1,8,1]{2,3,1,0:T(1,128)} %copy-done.13) | copy-start | bytes 12292
  189.5 2.7 %copy-start.10 = (f32[128,1,8,1]{2,3,1,0:T(1,128)S(1)}, f32[128,1,8,1]{2,3,1,0:T(1,128)}, u32[]{:S(2)}) copy-start(f32[128,1,8,1]{2,3,1,0:T(1,128)} %copy-done.9) | copy-start | bytes 12292
  190.2 17.8 %copy-start.16 = (f32[32,8,3]{1,2,0:T(4,128)S(1)}, f32[32,8,3]{1,2,0:T(4,128)}, u32[]{:S(2)}) copy-start(f32[32,8,3]{1,2,0:T(4,128)} %get-tuple-element.92) | copy-start | bytes 9220
  190.2 18.0 %copy-start.15 = (f32[32,8,3,3]{1,3,2,0:T(4,128)S(1)}, f32[32,8,3,3]{1,3,2,0:T(4,128)}, u32[]{:S(2)}) copy-start(f32[32,8,3,3]{1,3,2,0:T(4,128)} %get-tuple-element.93) | copy-start | bytes 27652
  190.2 18.0 %copy-start.18 = (pred[3,3]{1,0:T(4,128)(4,1)S(1)}, pred[3,3]{1,0:T(4,128)(4,1)}, u32[]{:S(2)}) copy-start(pred[3,3]{1,0:T(4,128)(4,1)} %copy-done.17) | copy-start | bytes 31
  190.2 18.2 %copy-start.4 = (f32[32,8,3,96]{3,1,2,0:T(8,128)S(1)}, f32[32,8,3,96]{3,1,2,0:T(8,128)}, u32[]{:S(2)}) copy-start(f32[32,8,3,96]{3,1,2,0:T(8,128)} %get-tuple-element.91) | copy-start | bytes 884740
  202.1 23.6 %all-to-all-start.1 = ((f32[128,1,8,1,128]{4,2,3,1,0:T(8,128)}), f32[128,1,8,1,128]{4,2,3,1,0:T(8,128)}, u32[]{:S(2)}, u32[]{:S(2)}) async-start(f32[128,1,8,1,128]{4,2,3,1,0:T(8,128)} %copy.61), calls=%async_computation.1 | async-start | bytes 1048576 | tf_op jit(solution)/shard_map/all_to_all | solution.py:92
  225.7 1.7 copy-start.19
  (2 other events, 1.1 us)
where the time goes:
time: 247 us; the launch traced here: 246 us
  waiting for transfers between devices  99.7 us (40%)
  blocking collectives  61.5 us (25%)
  starting transfers between devices  48.2 us (20%)
  local copies, waits for them, and re-layouts  13.9 us (6%)
  matrix products  12.3 us (5%)
  other arithmetic  9.94 us (4%)
    all_to_all x2, blocking collectives, shards(): lax.all_to_all(outgoing[:, :, :, step_index:step_index + 1], 'pre', split...  45.4 us
    all_to_all x3, waiting for transfers between devices, shards(): lax.all_to_all(owner_part, 'pre', split_axis=0, concat_axis=0, tiled=True)  39 us
    all_to_all x3, waiting for transfers between devices, shards(): lax.all_to_all(owner_sum, 'pre', split_axis=0, concat_axis=0, tiled=True)  27.1 us
    all_to_all x3, waiting for transfers between devices, shards(): lax.all_to_all(owner_max, 'pre', split_axis=0, concat_axis=0, tiled=True)  23 us
    all_to_all x3, starting transfers between devices, shards(): lax.all_to_all(owner_part, 'pre', split_axis=0, concat_axis=0, tiled=True)  16.1 us
    all_to_all x1, blocking collectives, shards(): lax.all_to_all(attended, 'head', split_axis=0, concat_axis=1, tiled=True)  16 us
    all_to_all x3, starting transfers between devices, shards(): lax.all_to_all(owner_sum, 'pre', split_axis=0, concat_axis=0, tiled=True)  13.9 us
    all_to_all x3, starting transfers between devices, shards(): lax.all_to_all(owner_max, 'pre', split_axis=0, concat_axis=0, tiled=True)  13.5 us
  transfers between devices with their start and end apart: 10, of which 10 were waited for; matrix products, arithmetic and copies ran while one was open for 11% of the time, Pallas kernels for 0%

commit v1 on v0

v1 whole, which is shorter than its diff:
```python
import math

import jax
import jax.numpy as jnp
from jax import lax
from jax.experimental import pallas as pl
from jax.experimental.pallas import tpu as pltpu
from jax.sharding import PartitionSpec as P

MESH = pl.DeviceIdType.MESH
masked_score = -1e30
offsets = (0, 1, 7, 2, 6, 3, 5, 4)
query_groups = ((0, 3), (3, 5))
return_groups = ((0, 3), (3, 2), (5, 2), (7, 1))


def dot_t(a, b):
    return lax.dot_general(a, b, (((1,), (1,)), ((), ())), preferred_element_type=jnp.float32)


def kernel(
    src_ref,
    slot_ref,
    len_ref,
    q4_hbm,
    q2_hbm,
    pk_hbm,
    pv_hbm,
    sk_hbm,
    sv_hbm,
    nk_hbm,
    nv_hbm,
    out_ref,
    q4,
    q2,
    kvk,
    kvv,
    sk,
    sv,
    nk,
    nv,
    qsend,
    qrecv,
    osend,
    orecv,
    ssend,
    srecv,
    snew,
    pnew,
    lpart,
    lmax,
    lsum,
    stage,
    load_sem,
    ring_send,
    ring_recv,
    q_send_sem,
    q_recv_sem,
    o_send_sem,
    o_recv_sem,
    s_send_sem,
    s_recv_sem,
    y_send_sem,
    y_recv_sem,
    own_sem,
):
    pre = lax.axis_index("pre")
    head = lax.axis_index("head")
    z = pre // 8
    me = pre % 8
    plane = z * 8
    right = ((z + 1) % 8) * 8 + me
    left = ((z + 7) % 8) * 8 + me
    to_log2 = 128 ** (-0.5) * math.log2(math.e)

    barrier = pltpu.get_barrier_semaphore()

    def greet(pre_index, head_index):
        pl.semaphore_signal(
            barrier, inc=1, device_id=(pre_index, head_index), device_id_type=MESH
        )

    greet(right, head)
    greet(left, head)
    for i in range(1, 8):
        greet(plane + (me + i) % 8, head)
    for i in range(1, 8):
        greet(pre, (head + i) % 8)

    loads = [
        pltpu.make_async_copy(a, b, load_sem.at[i])
        for i, (a, b) in enumerate(
            (
                (q4_hbm, q4),
                (q2_hbm, q2),
                (nk_hbm, nk),
                (nv_hbm, nv),
                (sk_hbm, sk),
                (sv_hbm, sv),
                (pk_hbm, kvk.at[0]),
                (pv_hbm, kvv.at[0]),
            )
        )
    ]
    for copy in loads:
        copy.start()

    def ring(way, hop, which):
        held, own = ((kvk, pk_hbm), (kvv, pv_hbm))[which]
        if way == 0:
            source, target, device = (9 - hop) % 8, 8 - hop, right
        else:
            source, target, device = hop - 1, hop, left
        return pltpu.make_async_remote_copy(
            src_ref=own if hop == 1 else held.at[source],
            dst_ref=held.at[target],
            send_sem=ring_send.at[way, hop - 1, which],
            recv_sem=ring_recv.at[way, hop - 1, which],
            device_id=(device, head),
            device_id_type=MESH,
        )

    def plane_copy(source, target, group, sends, receives, index, i):
        first, count = group
        peer = (me + i) % 8
        return pltpu.make_async_remote_copy(
            src_ref=source.at[pl.ds(first, count), peer],
            dst_ref=target.at[pl.ds(first, count), me],
            send_sem=sends.at[index, i],
            recv_sem=receives.at[index, i],
            device_id=(plane + peer, head),
            device_id_type=MESH,
        )

    def query_copy(index, i):
        return plane_copy(
            qsend, qrecv, query_groups[index], q_send_sem, q_recv_sem, index, i
        )

    def part_copy(index, i):
        return plane_copy(
            osend, orecv, return_groups[index], o_send_sem, o_recv_sem, index, i
        )

    def stat_copy(index, i):
        return plane_copy(
            ssend, srecv, return_groups[index], s_send_sem, s_recv_sem, index, i
        )

    pl.semaphore_wait(barrier, 16)
    for which in range(2):
        for way in range(2):
            ring(way, 1, which).start()

    loads[0].wait()

    def pack(k, carry):
        for d in range(8):
            first = q4[src_ref[k * 16 + d * 2]].astype(jnp.float32).reshape(24, 128)
            second = q4[src_ref[k * 16 + d * 2 + 1]].astype(jnp.float32).reshape(24, 128)
            qsend[k, d] = jnp.concatenate([first, second], axis=0).astype(jnp.bfloat16)
        return carry

    lax.fori_loop(0, 8, pack, 0)
    qrecv[:, me] = qsend[:, me]

    for index in range(2):
        for i in range(1, 8):
            query_copy(index, i).start()

    loads[1].wait()
    loads[2].wait()
    snew[...] = dot_t(q2[...], nk[...])
    loads[4].wait()
    loads[5].wait()

    def pair(i):
        rows = pl.ds(i * 48, 48)
        keys = pl.ds(i * 192, 192)
        scores = dot_t(q2[rows, :], sk[keys, :])
        row = lax.broadcasted_iota(jnp.int32, (48, 192), 0)
        lane = lax.broadcasted_iota(jnp.int32, (48, 192), 1)
        low = jnp.where(row < 24, 0, 96)
        high = jnp.where(row < 24, len_ref[2 * i], 96 + len_ref[2 * i + 1])
        scores = jnp.where((lane >= low) & (lane < high), scores, masked_score)
        row = lax.broadcasted_iota(jnp.int32, (48, 96), 0)
        lane = lax.broadcasted_iota(jnp.int32, (48, 96), 1)
        second = row >= 24
        place = lane - jnp.where(second, 2 * i + 1, 2 * i)
        within = jnp.where(second, row - 24, row)
        fresh_ok = (
            (place == 0)
            | ((place == 32) & (within >= 8))
            | ((place == 64) & (within >= 16))
        )
        fresh = jnp.where(fresh_ok, snew[rows, :], masked_score)
        top = jnp.maximum(
            jnp.max(scores, axis=1, keepdims=True), jnp.max(fresh, axis=1, keepdims=True)
        )
        scores = jnp.exp2((scores - top) * to_log2)
        fresh = jnp.exp2((fresh - top) * to_log2)
        lmax[rows, :] = top * to_log2
        lsum[rows, :] = jnp.sum(scores, axis=1, keepdims=True) + jnp.sum(
            fresh, axis=1, keepdims=True
        )
        pnew[rows, :] = fresh.astype(jnp.bfloat16)
        lpart[rows, :] = jnp.dot(
            scores.astype(jnp.bfloat16), sv[keys, :], preferred_element_type=jnp.float32
        )

    def pairs(first):
        for j in range(4):
            pair(first + j)

    def pass_on(hop, which):
        for way in range(2):
            ring(way, hop, which).wait_recv()
            if hop < 3 or which == way:
                ring(way, hop + 1, which).start()

    pairs(0)
    pairs(4)
    pass_on(1, 0)
    pairs(8)
    pairs(12)
    pass_on(1, 1)
    loads[3].wait()
    part = lpart[...] + jnp.dot(pnew[...], nv[...], preferred_element_type=jnp.float32)
    lpart[...] = part / lsum[...]
    lmax[...] = lmax[...] + jnp.log2(lsum[...])

    def block(k):
        offset = offsets[k]
        scores = dot_t(qrecv[k].reshape(384, 128), kvk[offset])
        top = jnp.max(scores, axis=1, keepdims=True)
        scores = jnp.exp2((scores - top) * to_log2)
        total = jnp.sum(scores, axis=1, keepdims=True)
        part = jnp.dot(
            scores.astype(jnp.bfloat16), kvv[offset], preferred_element_type=jnp.float32
        )
        part = (part / total).astype(jnp.bfloat16).reshape(8, 48, 128)
        level = top * to_log2 + jnp.log2(total)
        row = lax.broadcasted_iota(jnp.int32, (48, 128), 0)
        lane = lax.broadcasted_iota(jnp.int32, (48, 128), 1)
        osend[k] = part
        for d in range(8):
            ssend[k, d] = jnp.sum(
                jnp.where(row == lane, level[d * 48 : d * 48 + 48], 0.0), axis=0, keepdims=True
            )
        orecv[k, me] = osend[k, me]
        srecv[k, me] = ssend[k, me]

    def send_back(index):
        for i in range(1, 8):
            part_copy(index, i).start()
            stat_copy(index, i).start()

    for i in range(1, 8):
        query_copy(0, i).wait_recv()
    loads[6].wait()
    loads[7].wait()
    block(0)
    block(1)
    block(2)
    send_back(0)
    pass_on(2, 0)
    pass_on(2, 1)
    for i in range(1, 8):
        query_copy(1, i).wait_recv()
    block(3)
    block(4)
    send_back(1)
    pass_on(3, 0)
    pass_on(3, 1)
    block(5)
    block(6)
    send_back(2)
    ring(0, 4, 0).wait_recv()
    ring(1, 4, 1).wait_recv()
    block(7)
    send_back(3)
    for index in range(4):
        for i in range(1, 8):
            part_copy(index, i).wait_recv()
            stat_copy(index, i).wait_recv()

    def head_copy(i):
        peer = (head + i) % 8
        return pltpu.make_async_remote_copy(
            src_ref=stage.at[peer],
            dst_ref=out_ref.at[head],
            send_sem=y_send_sem.at[i],
            recv_sem=y_recv_sem.at[i],
            device_id=(pre, peer),
            device_id_type=MESH,
        )

    def combine(target):
        parts = []
        levels = []
        row = lax.broadcasted_iota(jnp.int32, (24, 128), 0)
        lane = lax.broadcasted_iota(jnp.int32, (24, 128), 1)
        for j in range(4):
            slot = slot_ref[target * 4 + j]
            which = slot % 2
            both = orecv[slot // 16, (slot // 2) % 8].astype(jnp.float32)
            stats = srecv[slot // 16, (slot // 2) % 8]
            parts.append(jnp.where(row * 0 + which == 0, both[:24], both[24:]))
            levels.append(
                jnp.sum(
                    jnp.where(lane == row + 24 * which, stats, 0.0), axis=1, keepdims=True
                )
            )
        parts = jnp.concatenate(parts, axis=0)
        levels = jnp.concatenate(levels, axis=0)
        rows = pl.ds(pl.multiple_of(target * 96, 96), 96)
        local = lmax[rows, :]
        top = jnp.maximum(levels, local)
        pre_factor = jnp.exp2(levels - top)
        local_factor = jnp.exp2(local - top)
        mixed = (parts * pre_factor + lpart[rows, :] * local_factor) / (
            pre_factor + local_factor
        )
        stage[target] = mixed.astype(jnp.bfloat16)

    for batch in ((4, 3, 5, 2), (6, 1, 7, 0)):
        for i in batch:
            combine((head + i) % 8)
        for i in batch:
            if i:
                head_copy(i).start()
    own = pltpu.make_async_copy(stage.at[head], out_ref.at[head], own_sem)
    own.start()

    for hop in range(1, 5):
        for way in range(2):
            for which in range(2):
                if hop < 4 or which == way:
                    ring(way, hop, which).wait_send()
    for index in range(2):
        for i in range(1, 8):
            query_copy(index, i).wait_send()
    for index in range(4):
        for i in range(1, 8):
            part_copy(index, i).wait_send()
            stat_copy(index, i).wait_send()
    own.wait()
    for i in range(1, 8):
        head_copy(i).wait()


def shards(
    queries,
    prefix_keys,
    prefix_values,
    suffix_keys,
    suffix_values,
    new_keys,
    new_values,
    suffix_lengths,
    prefix_of_row,
    owner_of_prefix,
):
    bf16 = jnp.bfloat16
    plane = lax.axis_index("pre") // 8
    row_index = jnp.arange(32, dtype=jnp.int32)
    lookup = prefix_of_row[:, None] == jnp.arange(64, dtype=jnp.int32)[None, :]
    owner = jnp.sum(jnp.where(lookup, owner_of_prefix[None, :], 0), axis=1)
    earlier = (prefix_of_row[:, None] == prefix_of_row[None, :]) & (
        row_index[None, :] < row_index[:, None]
    )
    rank = jnp.sum(earlier.astype(jnp.int32), axis=1)
    offset = (owner // 8 - plane + 8) % 8
    place = jnp.where(offset == 0, 0, jnp.where(offset <= 4, 2 * offset - 1, 16 - 2 * offset))
    slot = place * 16 + (owner % 8) * 2 + rank
    match = slot[None, :] == jnp.arange(128, dtype=jnp.int32)[:, None]
    source = jnp.sum(jnp.where(match, row_index[None, :], 0), axis=1)

    by_step = jnp.transpose(queries, (0, 2, 1, 3))
    smem = pl.BlockSpec(memory_space=pltpu.SMEM)
    anywhere = pl.BlockSpec(memory_space=pltpu.HBM)
    dma = pltpu.SemaphoreType.DMA
    gathered = pl.pallas_call(
        kernel,
        out_shape=jax.ShapeDtypeStruct((8, 96, 128), bf16),
        in_specs=[smem] * 3 + [anywhere] * 8,
        out_specs=anywhere,
        scratch_shapes=[
            pltpu.VMEM((32, 3, 8, 128), bf16),
            pltpu.VMEM((768, 128), bf16),
            pltpu.VMEM((8, 512, 128), bf16),
            pltpu.VMEM((8, 512, 128), bf16),
            pltpu.VMEM((3072, 128), bf16),
            pltpu.VMEM((3072, 128), bf16),
            pltpu.VMEM((96, 128), bf16),
            pltpu.VMEM((96, 128), bf16),
            pltpu.VMEM((8, 8, 48, 128), bf16),
            pltpu.VMEM((8, 8, 48, 128), bf16),
            pltpu.VMEM((8, 8, 48, 128), bf16),
            pltpu.VMEM((8, 8, 48, 128), bf16),
            pltpu.VMEM((8, 8, 1, 128), jnp.float32),
            pltpu.VMEM((8, 8, 1, 128), jnp.float32),
            pltpu.VMEM((768, 96), jnp.float32),
            pltpu.VMEM((768, 96), bf16),
            pltpu.VMEM((768, 128), jnp.float32),
            pltpu.VMEM((768, 1), jnp.float32),
            pltpu.VMEM((768, 1), jnp.float32),
            pltpu.VMEM((8, 96, 128), bf16),
            dma((8,)),
            dma((2, 4, 2)),
            dma((2, 4, 2)),
            dma((2, 8)),
            dma((2, 8)),
            dma((4, 8)),
            dma((4, 8)),
            dma((4, 8)),
            dma((4, 8)),
            dma((8,)),
            dma((8,)),
            dma,
        ],
        compiler_params=pltpu.CompilerParams(
            collective_id=0, has_side_effects=True, vmem_limit_bytes=60 * 1024 * 1024
        ),
        cost_estimate=pl.CostEstimate(
            flops=1_200_000_000, bytes_accessed=3_000_000, transcendentals=1_800_000
        ),
        name="shared_prefix",
    )(
        source,
        slot,
        suffix_lengths,
        by_step,
        by_step.reshape(768, 128),
        prefix_keys.reshape(512, 128),
        prefix_values.reshape(512, 128),
        suffix_keys.reshape(3072, 128),
        suffix_values.reshape(3072, 128),
        jnp.transpose(new_keys, (1, 2, 0, 3)).reshape(96, 128),
        jnp.transpose(new_values, (1, 2, 0, 3)).reshape(96, 128),
    )
    ordered = jnp.transpose(gathered.reshape(8, 4, 3, 8, 128), (1, 0, 3, 2, 4))
    return ordered.reshape(4, 64, 3, 128)


def solution(mesh):
    in_specs = (
        P("pre", "head", None, None),
        P("pre", None, "head", None),
        P("pre", None, "head", None),
        P("pre", None, "head", None),
        P("pre", None, "head", None),
        P("pre", None, "head", None),
        P("pre", None, "head", None),
        P("pre"),
        P("pre"),
        P(),
    )
    out_specs = P(("pre", "head"), None, None, None)
    return jax.shard_map(shards, mesh=mesh, in_specs=in_specs, out_specs=out_specs, check_vma=False)
```

time: 247 us -> 56.8 us (0.23)
  waiting for transfers between devices: 99.7 us -> 0 us
  blocking collectives: 61.5 us -> 0 us
  Pallas kernels: 0 us -> 53.3 us
  starting transfers between devices: 48.2 us -> 0 us
  matrix products: 12.3 us -> 0 us
  local copies, waits for them, and re-layouts: 13.9 us -> 2.32 us
  other arithmetic: 9.94 us -> 0.98 us
    all_to_all x10 -> x0, waiting for transfers between devices: 99.7 us -> none  [the longest x3 39 us: shards(): lax.all_to_all(owner_part, 'pre', split_axis=0, concat_axis=0, tiled=True)]
    all_to_all x3 -> x0, blocking collectives: 61.5 us -> none  [the longest x2 45.4 us: shards(): lax.all_to_all(outgoing[:, :, :, step_index:step_index + 1], 'pre', split...]
    pallas_call x0 -> x1, Pallas kernels: none -> 53.3 us  [shards(): pl.pallas_call(kernel, out_shape=jax.ShapeDtypeStruct((8, 96, 128), bf16)...]
    all_to_all x10 -> x0, starting transfers between devices: 48.2 us -> none  [the longest x3 16.1 us: shards(): lax.all_to_all(owner_part, 'pre', split_axis=0, concat_axis=0, tiled=True)]
    dot_general x10 -> x0, matrix products: 12.3 us -> none  [the longest x3 3.35 us: score_block(): jnp.dot(expo.astype(jnp.bfloat16), prefix_value, preferred_element_type=j...]
    reduce_sum x8 -> x3, other arithmetic: 6.05 us -> 0.95 us  [the longest x1 0.6 us: shards(): source = jnp.sum(jnp.where(match, row_index[None, :], 0), axis=1)]
    another operation x6 -> x0, local copies, waits for them, and re-layouts: 4.29 us -> none  [the longest x3 2.15 us: shards(): owner_max = jnp.stack(max_list, axis=1)]
    gather x4 -> x0, local copies, waits for them, and re-layouts: 3.49 us -> none  [the longest x1 1.68 us: shards(): jnp.take(grouped, source, axis=0)]
  transfers between devices with their start and end apart: 10 -> 0, of which waited for: 10 -> 0; matrix products, arithmetic and copies ran while one was open for 11% -> 0% of each run, Pallas kernels for 0% -> 0%
where the time goes in v1:
time: 56.8 us; the launch traced here: 56.6 us
  Pallas kernels  53.3 us (94%)
  local copies, waits for them, and re-layouts  2.32 us (4%)
  other arithmetic  0.98 us (2%)
    pallas_call x1, Pallas kernels, shards(): pl.pallas_call(kernel, out_shape=jax.ShapeDtypeStruct((8, 96, 128), bf16)...  53.3 us
    transpose x1, local copies, waits for them, and re-layouts, shards(): ordered = jnp.transpose(gathered.reshape(8, 4, 3, 8, 128), (1, 0, 3, 2, 4))  1.65 us

profile of v1, /device:TPU:1, one launch (start us, length us, event | category | flops | bytes accessed | tf_op | source)
XLA Modules:
  0.0 56.6 jit_solution(11741152486608476185)
XLA Ops:
  0.0 0.0 copy-start.1
  0.0 0.0 copy-start.2
  0.0 0.7 %copy-done.1 = s32[64]{0:T(128)S(1)} copy-done((s32[64]{0:T(128)S(1)}, s32[64]{0:T(128)}, u32[]{:S(2)}) %copy-start.1) | copy-done | bytes 280
  0.7 0.0 copy-done.2
  0.7 0.2 select_reduce_fusion.1
  0.8 0.2 convert_reduce_fusion
  1.1 0.0 copy-start
  1.1 0.6 %select_reduce_fusion.src_ref = s32[128]{0:T(128)} fusion(s32[32]{0:T(128)S(1)} %fusion.5.slot_ref), kind=kLoop, calls=%fused_computation.1 | loop fusion | flops 12160 | bytes 640 | tf_op jit(solution)/shard_map/reduce_sum | solution.py:377
  1.7 0.0 copy-done
  1.7 53.3 %shared_prefix.1 = bf16[8,96,128]{2,1,0:T(8,128)(2,1)} custom-call(s32[128]{0:T(128)} %select_reduce_fusion.src_ref, s32[32]{0:T(128)} %copy-done, s32[32]{0:T(128)} %len_ref.1, bf16[32,3,8,128]{3,2,1,0:T(8,128)(2,1)} %bitcast.22, bf16[768,128]{1,0:T(8,128)(2,1)} %bitcast.23, bf16[512,128]{1,0:T(8,128)(2,1)} %bitcast.24, bf16[512,128]{1,0:T(8,128)(2,1)} %bitcast.25, ...), custom_call_target="tpu_custom_call" | custom-call | flops 1200000000 | bytes 3000000 | tf_op jit(solution)/shard_map/shared_prefix/pallas_call | solution.py:383
  54.9 1.7 %copy.14 = bf16[4,8,8,3,128]{4,2,1,3,0:T(8,128)(2,1)} copy(bf16[4,8,8,3,128]{4,2,3,0,1:T(8,128)(2,1)} %bitcast.19) | data formatting | bytes 393216 | tf_op jit(solution)/shard_map/transpose | solution.py:442
  (1 shorter events, 0.0 us)
Async XLA Ops:
  0.0 0.7 %copy-start.1 = (s32[64]{0:T(128)S(1)}, s32[64]{0:T(128)}, u32[]{:S(2)}) copy-start(s32[64]{0:T(128)} %param.19) | copy-start | bytes 772
  0.0 0.7 %copy-start.2 = (s32[32]{0:T(128)S(1)}, s32[32]{0:T(128)}, u32[]{:S(2)}) copy-start(s32[32]{0:T(128)} %param.18) | copy-start | bytes 388
  1.1 0.6 %copy-start = (s32[32]{0:T(128)}, s32[32]{0:T(128)S(1)}, u32[]{:S(2)}) copy-start(s32[32]{0:T(128)S(1)} %fusion.5.slot_ref) | copy-start | bytes 388

commit v2 on v1

v2 whole, which is shorter than its diff:
```python
import math

import jax
import jax.numpy as jnp
from jax import lax
from jax.experimental import pallas as pl
from jax.experimental.pallas import tpu as pltpu
from jax.sharding import PartitionSpec as P

MESH = pl.DeviceIdType.MESH
masked_score = -1e30
offsets = (0, 1, 7, 2, 6, 3, 5, 4)
return_groups = ((0, 3), (3, 2), (5, 2), (7, 1))


def dot_t(a, b):
    return lax.dot_general(a, b, (((1,), (1,)), ((), ())), preferred_element_type=jnp.float32)


def kernel(
    prefix_hbm,
    owner_hbm,
    len_hbm,
    q4_hbm,
    q2_hbm,
    pk_hbm,
    pv_hbm,
    sk_hbm,
    sv_hbm,
    nk_hbm,
    nv_hbm,
    out_ref,
    prefix_here,
    owner_here,
    len_ref,
    index_rows,
    index_ref,
    qall,
    q2,
    kvk,
    kvv,
    sk,
    sv,
    nk,
    nv,
    qpack,
    osend,
    orecv,
    ssend,
    srecv,
    snew,
    pnew,
    lpart,
    lmax,
    lsum,
    weights,
    inverse,
    stage,
    load_sem,
    ring_send,
    ring_recv,
    q_send_sem,
    q_recv_sem,
    index_sem,
    o_send_sem,
    o_recv_sem,
    s_send_sem,
    s_recv_sem,
    y_send_sem,
    y_recv_sem,
    own_sem,
):
    pre = lax.axis_index("pre")
    head = lax.axis_index("head")
    z = pre // 8
    me = pre % 8
    plane = z * 8
    right = ((z + 1) % 8) * 8 + me
    left = ((z + 7) % 8) * 8 + me
    column, core = me // 2, me % 2
    ahead = ((column + 1) % 4) * 2 + core
    behind = ((column + 3) % 4) * 2 + core
    opposite = ((column + 2) % 4) * 2 + core
    sibling = column * 2 + 1 - core
    to_log2 = 128 ** (-0.5) * math.log2(math.e)

    barrier = pltpu.get_barrier_semaphore()

    def greet(pre_index, head_index):
        pl.semaphore_signal(
            barrier, inc=1, device_id=(pre_index, head_index), device_id_type=MESH
        )

    greet(right, head)
    greet(left, head)
    for i in range(1, 8):
        greet(plane + (me + i) % 8, head)
    for i in range(1, 8):
        greet(pre, (head + i) % 8)

    loads = [
        pltpu.make_async_copy(a, b, load_sem.at[i])
        for i, (a, b) in enumerate(
            (
                (prefix_hbm, prefix_here),
                (owner_hbm, owner_here),
                (len_hbm, len_ref),
                (q4_hbm, qall.at[me, pl.ds(0, 32)]),
                (q2_hbm, q2),
                (nk_hbm, nk),
                (nv_hbm, nv),
                (sk_hbm, sk),
                (sv_hbm, sv),
                (pk_hbm, kvk.at[0]),
                (pv_hbm, kvv.at[0]),
            )
        )
    ]
    for copy in loads:
        copy.start()

    def ring(way, hop, which):
        held, own = ((kvk, pk_hbm), (kvv, pv_hbm))[which]
        if way == 0:
            source, target, device = (9 - hop) % 8, 8 - hop, right
        else:
            source, target, device = hop - 1, hop, left
        return pltpu.make_async_remote_copy(
            src_ref=own if hop == 1 else held.at[source],
            dst_ref=held.at[target],
            send_sem=ring_send.at[which],
            recv_sem=ring_recv.at[way, hop - 1, which],
            device_id=(device, head),
            device_id_type=MESH,
        )

    def plane_copy(source, target, blocks, send_sem, recv_sem, i):
        peer = (me + i) % 8
        return pltpu.make_async_remote_copy(
            src_ref=source.at[blocks, peer],
            dst_ref=target.at[blocks, me],
            send_sem=send_sem,
            recv_sem=recv_sem,
            device_id=(plane + peer, head),
            device_id_type=MESH,
        )

    def wait_for(block, sem):
        pltpu.make_async_copy(block, block, sem).wait()

    def query_copy(i, source, rows, peer):
        block = qall.at[source, rows]
        return pltpu.make_async_remote_copy(
            src_ref=block,
            dst_ref=block,
            send_sem=q_send_sem.at[i],
            recv_sem=q_recv_sem.at[i],
            device_id=(plane + peer, head),
            device_id_type=MESH,
        )

    every, first_half, second_half = pl.ds(0, 33), pl.ds(0, 16), pl.ds(16, 17)

    seven = pl.ds(0, 7)

    def part_copy(index, i):
        blocks = pl.ds(*return_groups[index])
        return plane_copy(osend, orecv, blocks, o_send_sem.at[index], o_recv_sem.at[index], i)

    def stat_copy(i):
        return plane_copy(ssend, srecv, pl.ds(0, 8), s_send_sem, s_recv_sem, i)

    pl.semaphore_wait(barrier, 16)
    for way in range(2):
        ring(way, 1, 0).start()

    query_sends = [
        query_copy(0, me, every, ahead),
        query_copy(1, me, every, behind),
        query_copy(2, me, every, sibling),
        query_copy(3, behind, first_half, ahead),
        query_copy(4, behind, every, sibling),
        query_copy(5, ahead, second_half, behind),
        query_copy(6, ahead, every, sibling),
        query_copy(7, opposite, first_half, sibling),
        query_copy(8, opposite, second_half, sibling),
    ]
    loads[0].wait()
    qall[me, 32] = jnp.full((3, 8, 128), -1.0, jnp.bfloat16)
    qall[me, 32, 0, :, 0:32] = jnp.broadcast_to(prefix_here[...], (8, 32)).astype(jnp.bfloat16)
    loads[3].wait()
    for copy in query_sends[:3]:
        copy.start()

    loads[1].wait()

    def small_dot(a, b):
        return jnp.dot(
            a.astype(jnp.bfloat16), b.astype(jnp.bfloat16), preferred_element_type=jnp.float32
        )

    def iota(shape, dim):
        return lax.broadcasted_iota(jnp.int32, shape, dim)

    def ones_where(condition):
        return jnp.where(condition, 1.0, 0.0)

    def owner_at(k):
        offset = jnp.where((k & 1) == 1, (k + 1) >> 1, 8 - (k >> 1))
        return ((z + offset) & 7) * 8

    def named_by(d):
        names = qall[d, 32, 0].astype(jnp.float32)[0:1]
        return ones_where(names == iota((64, 128), 0).astype(jnp.float32))

    before = ones_where(iota((128, 128), 0) < iota((128, 128), 1))
    place = iota((64, 64), 0)
    owners = owner_here[...]
    held = ones_where(owners == owner_at(place >> 3) + (place & 7))
    mine = small_dot(held, named_by(me))
    earlier = small_dot(mine, before)
    slots = small_dot(2 * iota((8, 64), 1).astype(jnp.float32), mine) + small_dot(
        jnp.ones((8, 64), jnp.float32), mine * earlier
    )
    index_rows[16:24, :] = slots.astype(jnp.int32)

    loads[4].wait()
    loads[5].wait()
    snew[...] = dot_t(q2[...], nk[...])
    loads[2].wait()
    loads[7].wait()
    loads[8].wait()

    def pair(i):
        rows = pl.ds(i * 48, 48)
        keys = pl.ds(i * 192, 192)
        scores = dot_t(q2[rows, :], sk[keys, :])
        row = lax.broadcasted_iota(jnp.int32, (48, 192), 0)
        lane = lax.broadcasted_iota(jnp.int32, (48, 192), 1)
        low = jnp.where(row < 24, 0, 96)
        high = jnp.where(row < 24, len_ref[0, 2 * i], 96 + len_ref[0, 2 * i + 1])
        scores = jnp.where((lane >= low) & (lane < high), scores, masked_score)
        row = lax.broadcasted_iota(jnp.int32, (48, 96), 0)
        lane = lax.broadcasted_iota(jnp.int32, (48, 96), 1)
        second = row >= 24
        place = lane - jnp.where(second, 2 * i + 1, 2 * i)
        within = jnp.where(second, row - 24, row)
        fresh_ok = (
            (place == 0)
            | ((place == 32) & (within >= 8))
            | ((place == 64) & (within >= 16))
        )
        fresh = jnp.where(fresh_ok, snew[rows, :], masked_score)
        top = jnp.maximum(
            jnp.max(scores, axis=1, keepdims=True), jnp.max(fresh, axis=1, keepdims=True)
        )
        scores = jnp.exp2((scores - top) * to_log2)
        fresh = jnp.exp2((fresh - top) * to_log2)
        lmax[rows, :] = top * to_log2
        lsum[rows, :] = jnp.sum(scores, axis=1, keepdims=True) + jnp.sum(
            fresh, axis=1, keepdims=True
        )
        pnew[rows, :] = fresh.astype(jnp.bfloat16)
        lpart[rows, :] = jnp.dot(
            scores.astype(jnp.bfloat16), sv[keys, :], preferred_element_type=jnp.float32
        )

    def pairs(first):
        for j in range(4):
            pair(first + j)

    def pass_on(hop, which):
        for way in range(2):
            ring(way, hop, which).wait_recv()
            if hop < 3 or which == way:
                ring(way, hop + 1, which).start()

    pairs(0)
    for way in range(2):
        ring(way, 1, 1).start()
    pairs(4)
    pass_on(1, 0)
    pairs(8)
    query_sends[0].wait_recv()
    query_sends[3].start()
    query_sends[4].start()
    query_sends[1].wait_recv()
    query_sends[5].start()
    query_sends[6].start()
    pairs(12)
    loads[6].wait()
    part = lpart[...] + jnp.dot(pnew[...], nv[...], preferred_element_type=jnp.float32)
    lpart[...] = part / lsum[...]
    lmax[...] = lmax[...] + jnp.log2(lsum[...])

    def index_at(table, place, last):
        return jnp.minimum(jnp.maximum(index_ref[table * 8, place], 0), last)

    def weigh(k):
        for d in range(8):
            rows = [qall[d, index_at(rank, d * 8 + k, 31)] for rank in range(2)]
            both = [row.astype(jnp.float32).reshape(24, 128) for row in rows]
            qpack[k, d] = jnp.concatenate(both, axis=0).astype(jnp.bfloat16)
        scores = dot_t(qpack[k].reshape(384, 128), kvk[offsets[k]])
        top = jnp.max(scores, axis=1, keepdims=True)
        scores = jnp.exp2((scores - top) * to_log2)
        total = jnp.sum(scores, axis=1, keepdims=True)
        weights[k] = scores.astype(jnp.bfloat16)
        inverse[k] = 1.0 / total
        level = top * to_log2 + jnp.log2(total)
        row = iota((48, 128), 0)
        lane = iota((48, 128), 1)
        for d in range(8):
            ssend[k, d] = jnp.sum(
                jnp.where(row == lane, level[d * 48 : d * 48 + 48], 0.0), axis=0, keepdims=True
            )
        srecv[k, me] = ssend[k, me]

    def blend(k):
        part = jnp.dot(weights[k], kvv[offsets[k]], preferred_element_type=jnp.float32)
        osend[k] = (part * inverse[k]).astype(jnp.bfloat16).reshape(8, 48, 128)
        orecv[k, me] = osend[k, me]

    def send_back(index):
        for i in range(1, 8):
            part_copy(index, i).start()

    pass_on(1, 1)
    query_sends[3].wait_recv()
    query_sends[7].start()
    query_sends[5].wait_recv()
    query_sends[8].start()
    pass_on(2, 0)
    for i in (2, 4, 6, 7, 8):
        query_sends[i].wait_recv()
    here = ones_where(owners == owner_at(iota((8, 64), 0)) + me)
    match = jnp.concatenate(
        [small_dot(here, named_by(d)) for d in range(8)], axis=0
    )
    earlier = small_dot(match, before)
    numbers = iota((8, 128), 1).astype(jnp.bfloat16)
    for rank in range(2):
        chosen = jnp.where(earlier == rank, match, 0.0).astype(jnp.bfloat16)
        index_rows[rank * 8 : rank * 8 + 8, 0:64] = dot_t(numbers, chosen).astype(jnp.int32)
    index_copy = pltpu.make_async_copy(index_rows, index_ref, index_sem)
    index_copy.start()
    index_copy.wait()
    loads[9].wait()
    loads[10].wait()
    weigh(0)
    blend(0)
    weigh(1)
    weigh(2)
    blend(1)
    blend(2)
    send_back(0)
    weigh(3)
    weigh(4)
    pass_on(2, 1)
    blend(3)
    blend(4)
    send_back(1)
    pass_on(3, 0)
    weigh(5)
    weigh(6)
    pass_on(3, 1)
    blend(5)
    blend(6)
    send_back(2)
    ring(0, 4, 0).wait_recv()
    weigh(7)
    for i in range(1, 8):
        stat_copy(i).start()
    ring(1, 4, 1).wait_recv()
    blend(7)
    send_back(3)
    for index in range(4):
        wait_for(orecv.at[pl.ds(*return_groups[index]), seven], o_recv_sem.at[index])
    wait_for(srecv.at[:, seven], s_recv_sem)

    def head_copy(i):
        peer = (head + i) % 8
        return pltpu.make_async_remote_copy(
            src_ref=stage.at[peer],
            dst_ref=out_ref.at[head],
            send_sem=y_send_sem,
            recv_sem=y_recv_sem,
            device_id=(pre, peer),
            device_id_type=MESH,
        )

    def combine(target):
        parts = []
        levels = []
        row = lax.broadcasted_iota(jnp.int32, (24, 128), 0)
        lane = lax.broadcasted_iota(jnp.int32, (24, 128), 1)
        for j in range(4):
            slot = index_at(2, target * 4 + j, 127)
            which = slot % 2
            both = orecv[slot // 16, (slot // 2) % 8].astype(jnp.float32)
            stats = srecv[slot // 16, (slot // 2) % 8]
            parts.append(jnp.where(row * 0 + which == 0, both[:24], both[24:]))
            levels.append(
                jnp.sum(
                    jnp.where(lane == row + 24 * which, stats, 0.0), axis=1, keepdims=True
                )
            )
        parts = jnp.concatenate(parts, axis=0)
        levels = jnp.concatenate(levels, axis=0)
        rows = pl.ds(pl.multiple_of(target * 96, 96), 96)
        local = lmax[rows, :]
        top = jnp.maximum(levels, local)
        pre_factor = jnp.exp2(levels - top)
        local_factor = jnp.exp2(local - top)
        mixed = (parts * pre_factor + lpart[rows, :] * local_factor) / (
            pre_factor + local_factor
        )
        stage[target] = mixed.astype(jnp.bfloat16)

    for batch in ((4, 3, 5, 2), (6, 1, 7, 0)):
        for i in batch:
            combine((head + i) % 8)
        for i in batch:
            if i:
                head_copy(i).start()
    own = pltpu.make_async_copy(stage.at[head], out_ref.at[head], own_sem)
    own.start()

    for which in range(2):
        wait_for((kvk, kvv)[which].at[seven], ring_send.at[which])
    for copy in query_sends:
        copy.wait_send()
    for index in range(4):
        wait_for(osend.at[pl.ds(*return_groups[index]), seven], o_send_sem.at[index])
    wait_for(ssend.at[:, seven], s_send_sem)
    wait_for(stage.at[seven], y_send_sem)
    own.wait()
    wait_for(out_ref.at[seven], y_recv_sem)


def shards(
    queries,
    prefix_keys,
    prefix_values,
    suffix_keys,
    suffix_values,
    new_keys,
    new_values,
    suffix_lengths,
    prefix_of_row,
    owner_of_prefix,
):
    bf16 = jnp.bfloat16
    by_step = jnp.transpose(queries, (0, 2, 1, 3))
    anywhere = pl.BlockSpec(memory_space=pltpu.HBM)
    dma = pltpu.SemaphoreType.DMA
    gathered = pl.pallas_call(
        kernel,
        out_shape=jax.ShapeDtypeStruct((8, 96, 128), bf16),
        in_specs=[anywhere] * 11,
        out_specs=anywhere,
        scratch_shapes=[
            pltpu.VMEM((1, 32), jnp.int32),
            pltpu.VMEM((1, 64), jnp.int32),
            pltpu.SMEM((1, 32), jnp.int32),
            pltpu.VMEM((24, 128), jnp.int32),
            pltpu.SMEM((24, 128), jnp.int32),
            pltpu.VMEM((8, 33, 3, 8, 128), bf16),
            pltpu.VMEM((768, 128), bf16),
            pltpu.VMEM((8, 512, 128), bf16),
            pltpu.VMEM((8, 512, 128), bf16),
            pltpu.VMEM((3072, 128), bf16),
            pltpu.VMEM((3072, 128), bf16),
            pltpu.VMEM((96, 128), bf16),
            pltpu.VMEM((96, 128), bf16),
            pltpu.VMEM((8, 8, 48, 128), bf16),
            pltpu.VMEM((8, 8, 48, 128), bf16),
            pltpu.VMEM((8, 8, 48, 128), bf16),
            pltpu.VMEM((8, 8, 1, 128), jnp.float32),
            pltpu.VMEM((8, 8, 1, 128), jnp.float32),
            pltpu.VMEM((768, 96), jnp.float32),
            pltpu.VMEM((768, 96), bf16),
            pltpu.VMEM((768, 128), jnp.float32),
            pltpu.VMEM((768, 1), jnp.float32),
            pltpu.VMEM((768, 1), jnp.float32),
            pltpu.VMEM((8, 384, 512), bf16),
            pltpu.VMEM((8, 384, 1), jnp.float32),
            pltpu.VMEM((8, 96, 128), bf16),
            dma((11,)),
            dma((2,)),
            dma((2, 4, 2)),
            dma((9,)),
            dma((9,)),
            dma,
            dma((4,)),
            dma((4,)),
            dma,
            dma,
            dma,
            dma,
            dma,
        ],
        compiler_params=pltpu.CompilerParams(
            collective_id=0, has_side_effects=True, vmem_limit_bytes=60 * 1024 * 1024
        ),
        cost_estimate=pl.CostEstimate(
            flops=1_200_000_000, bytes_accessed=3_000_000, transcendentals=1_800_000
        ),
        name="shared_prefix",
    )(
        prefix_of_row.reshape(1, 32),
        owner_of_prefix.reshape(1, 64),
        suffix_lengths.reshape(1, 32),
        by_step,
        by_step.reshape(768, 128),
        prefix_keys.reshape(512, 128),
        prefix_values.reshape(512, 128),
        suffix_keys.reshape(3072, 128),
        suffix_values.reshape(3072, 128),
        jnp.transpose(new_keys, (1, 2, 0, 3)).reshape(96, 128),
        jnp.transpose(new_values, (1, 2, 0, 3)).reshape(96, 128),
    )
    ordered = jnp.transpose(gathered.reshape(8, 4, 3, 8, 128), (1, 0, 3, 2, 4))
    return ordered.reshape(4, 64, 3, 128)


def solution(mesh):
    in_specs = (
        P("pre", "head", None, None),
        P("pre", None, "head", None),
        P("pre", None, "head", None),
        P("pre", None, "head", None),
        P("pre", None, "head", None),
        P("pre", None, "head", None),
        P("pre", None, "head", None),
        P("pre"),
        P("pre"),
        P(),
    )
    out_specs = P(("pre", "head"), None, None, None)
    return jax.shard_map(shards, mesh=mesh, in_specs=in_specs, out_specs=out_specs, check_vma=False)
```

time: 56.8 us -> 54.5 us (0.960)
  other arithmetic: 0.98 us -> 0 us
  local copies, waits for them, and re-layouts: 2.32 us -> 1.65 us
  Pallas kernels: 53.3 us -> 52.7 us
    reduce_sum x3 -> x0, other arithmetic: 0.95 us -> none  [the longest x1 0.6 us: shards(): source = jnp.sum(jnp.where(match, row_index[None, :], 0), axis=1)]
    unnamed x6 -> x0, local copies, waits for them, and re-layouts: 0.67 us -> none
where the time goes in v2:
time: 54.5 us; the launch traced here: 54.4 us
  Pallas kernels  52.7 us (97%)
  local copies, waits for them, and re-layouts  1.65 us (3%)
    pallas_call x1, Pallas kernels, shards(): pl.pallas_call(kernel, out_shape=jax.ShapeDtypeStruct((8, 96, 128), bf16)...  52.7 us
    transpose x1, local copies, waits for them, and re-layouts, shards(): ordered = jnp.transpose(gathered.reshape(8, 4, 3, 8, 128), (1, 0, 3, 2, 4))  1.65 us

profile of v2, /device:TPU:1, one launch (start us, length us, event | category | flops | bytes accessed | tf_op | source)
XLA Modules:
  0.0 54.4 jit_solution(4402741207578095111)
XLA Ops:
  0.0 52.7 %shared_prefix.1 = bf16[8,96,128]{2,1,0:T(8,128)(2,1)} custom-call(s32[1,32]{1,0:T(1,128)} %bitcast.31, s32[1,64]{1,0:T(1,128)} %bitcast.32, s32[1,32]{1,0:T(1,128)} %bitcast.33, bf16[32,3,8,128]{3,2,1,0:T(8,128)(2,1)} %bitcast.25, bf16[768,128]{1,0:T(8,128)(2,1)} %bitcast.26, bf16[512,128]{1,0:T(8,128)(2,1)} %bitcast.27, bf16[512,128]{1,0:T(8,128)(2,1)} %bitcast.28, ...), custom_call_target="tpu_custom_call" | custom-call | flops 1200000000 | bytes 3000000 | tf_op jit(solution)/shard_map/shared_prefix/pallas_call | solution.py:457
  52.7 1.7 %copy.13 = bf16[4,8,8,3,128]{4,2,1,3,0:T(8,128)(2,1)} copy(bf16[4,8,8,3,128]{4,2,3,0,1:T(8,128)(2,1)} %bitcast.22) | data formatting | bytes 393216 | tf_op jit(solution)/shard_map/transpose | solution.py:523

commit v3 on v2

--- a/solution.py
+++ b/solution.py
@@ -69,6 +69,8 @@
     y_send_sem,
     y_recv_sem,
     own_sem,
+    above_here,
+    below_here,
 ):
     pre = lax.axis_index("pre")
     head = lax.axis_index("head")
@@ -91,12 +93,11 @@
             barrier, inc=1, device_id=(pre_index, head_index), device_id_type=MESH
         )
 
-    greet(right, head)
-    greet(left, head)
-    for i in range(1, 8):
-        greet(plane + (me + i) % 8, head)
-    for i in range(1, 8):
-        greet(pre, (head + i) % 8)
+    above, below = (head + 1) % 8, (head + 7) % 8
+    for peer in (right, left, plane + ahead, plane + behind, plane + sibling):
+        greet(peer, head)
+    greet(pre, above)
+    greet(pre, below)
 
     loads = [
         pltpu.make_async_copy(a, b, load_sem.at[i])
@@ -170,9 +171,18 @@
     def stat_copy(i):
         return plane_copy(ssend, srecv, pl.ds(0, 8), s_send_sem, s_recv_sem, i)
 
-    pl.semaphore_wait(barrier, 16)
+    pl.semaphore_wait(barrier, 7)
     for way in range(2):
         ring(way, 1, 0).start()
+
+    def token(from_above, step):
+        tokens, peer = (above_here, below) if from_above else (below_here, above)
+        pl.semaphore_signal(
+            tokens.at[step], inc=1, device_id=(pre, peer), device_id_type=MESH
+        )
+
+    token(True, 0)
+    token(False, 0)
 
     query_sends = [
         query_copy(0, me, every, ahead),
@@ -357,6 +367,10 @@
     weigh(3)
     weigh(4)
     pass_on(2, 1)
+    pl.semaphore_wait(above_here.at[0], 1)
+    token(True, 1)
+    pl.semaphore_wait(below_here.at[0], 1)
+    token(False, 1)
     blend(3)
     blend(4)
     send_back(1)
@@ -364,6 +378,9 @@
     weigh(5)
     weigh(6)
     pass_on(3, 1)
+    pl.semaphore_wait(above_here.at[1], 1)
+    token(True, 2)
+    pl.semaphore_wait(below_here.at[1], 1)
     blend(5)
     blend(6)
     send_back(2)
@@ -417,6 +434,7 @@
         )
         stage[target] = mixed.astype(jnp.bfloat16)
 
+    pl.semaphore_wait(above_here.at[2], 1)
     for batch in ((4, 3, 5, 2), (6, 1, 7, 0)):
         for i in batch:
             combine((head + i) % 8)
@@ -499,6 +517,8 @@
             dma,
             dma,
             dma,
+            pltpu.SemaphoreType.REGULAR((3,)),
+            pltpu.SemaphoreType.REGULAR((2,)),
         ],
         compiler_params=pltpu.CompilerParams(
             collective_id=0, has_side_effects=True, vmem_limit_bytes=60 * 1024 * 1024

time: 54.5 us -> 52 us (0.954)
  Pallas kernels: 52.7 us -> 50 us
    pallas_call x1, Pallas kernels: 52.7 us -> 50 us  [shards(): pl.pallas_call(kernel, out_shape=jax.ShapeDtypeStruct((8, 96, 128), bf16)...]
where the time goes in v3:
time: 52 us; the launch traced here: 51.7 us
  Pallas kernels  50 us (96%)
  local copies, waits for them, and re-layouts  1.65 us (3%)
    pallas_call x1, Pallas kernels, shards(): pl.pallas_call(kernel, out_shape=jax.ShapeDtypeStruct((8, 96, 128), bf16)...  50 us
    transpose x1, local copies, waits for them, and re-layouts, shards(): ordered = jnp.transpose(gathered.reshape(8, 4, 3, 8, 128), (1, 0, 3, 2, 4))  1.65 us

profile of v3, /device:TPU:1, one launch (start us, length us, event | category | flops | bytes accessed | tf_op | source)
XLA Modules:
  0.0 51.7 jit_solution(13382419593698807112)
XLA Ops:
  0.0 50.0 %shared_prefix.1 = bf16[8,96,128]{2,1,0:T(8,128)(2,1)} custom-call(s32[1,32]{1,0:T(1,128)} %bitcast.31, s32[1,64]{1,0:T(1,128)} %bitcast.32, s32[1,32]{1,0:T(1,128)} %bitcast.33, bf16[32,3,8,128]{3,2,1,0:T(8,128)(2,1)} %bitcast.25, bf16[768,128]{1,0:T(8,128)(2,1)} %bitcast.26, bf16[512,128]{1,0:T(8,128)(2,1)} %bitcast.27, bf16[512,128]{1,0:T(8,128)(2,1)} %bitcast.28, ...), custom_call_target="tpu_custom_call" | custom-call | flops 1200000000 | bytes 3000000 | tf_op jit(solution)/shard_map/shared_prefix/pallas_call | solution.py:475
  50.0 1.7 %copy.13 = bf16[4,8,8,3,128]{4,2,1,3,0:T(8,128)(2,1)} copy(bf16[4,8,8,3,128]{4,2,3,0,1:T(8,128)(2,1)} %bitcast.22) | data formatting | bytes 393216 | tf_op jit(solution)/shard_map/transpose | solution.py:543

commit v4 on v3

--- a/solution.py
+++ b/solution.py
@@ -106,7 +106,7 @@
                 (prefix_hbm, prefix_here),
                 (owner_hbm, owner_here),
                 (len_hbm, len_ref),
-                (q4_hbm, qall.at[me, pl.ds(0, 32)]),
+                (q4_hbm, qall.at[me, pl.ds(1, 32)]),
                 (q2_hbm, q2),
                 (nk_hbm, nk),
                 (nv_hbm, nv),
@@ -117,8 +117,8 @@
             )
         )
     ]
-    for copy in loads:
-        copy.start()
+    for i in (0, 1, 3):
+        loads[i].start()
 
     def ring(way, hop, which):
         held, own = ((kvk, pk_hbm), (kvv, pv_hbm))[which]
@@ -160,7 +160,7 @@
             device_id_type=MESH,
         )
 
-    every, first_half, second_half = pl.ds(0, 33), pl.ds(0, 16), pl.ds(16, 17)
+    every, first_half, second_half = pl.ds(0, 33), pl.ds(0, 17), pl.ds(17, 16)
 
     seven = pl.ds(0, 7)
 
@@ -174,6 +174,8 @@
     pl.semaphore_wait(barrier, 7)
     for way in range(2):
         ring(way, 1, 0).start()
+    for i in (4, 5, 2, 7, 8, 6, 9, 10):
+        loads[i].start()
 
     def token(from_above, step):
         tokens, peer = (above_here, below) if from_above else (below_here, above)
@@ -185,21 +187,31 @@
     token(False, 0)
 
     query_sends = [
-        query_copy(0, me, every, ahead),
-        query_copy(1, me, every, behind),
-        query_copy(2, me, every, sibling),
-        query_copy(3, behind, first_half, ahead),
-        query_copy(4, behind, every, sibling),
-        query_copy(5, ahead, second_half, behind),
-        query_copy(6, ahead, every, sibling),
-        query_copy(7, opposite, first_half, sibling),
-        query_copy(8, opposite, second_half, sibling),
+        query_copy(0, me, first_half, ahead),
+        query_copy(1, me, first_half, behind),
+        query_copy(2, me, second_half, ahead),
+        query_copy(3, me, second_half, behind),
+        query_copy(4, me, every, sibling),
+        query_copy(5, behind, first_half, ahead),
+        query_copy(6, ahead, second_half, behind),
+        query_copy(7, behind, first_half, sibling),
+        query_copy(8, ahead, first_half, sibling),
+        query_copy(9, behind, second_half, sibling),
+        query_copy(10, ahead, second_half, sibling),
+        query_copy(11, opposite, first_half, sibling),
+        query_copy(12, opposite, second_half, sibling),
     ]
+
+    def hand_on(arrived, onward):
+        query_sends[arrived].wait_recv()
+        for i in onward:
+            query_sends[i].start()
+
     loads[0].wait()
-    qall[me, 32] = jnp.full((3, 8, 128), -1.0, jnp.bfloat16)
-    qall[me, 32, 0, :, 0:32] = jnp.broadcast_to(prefix_here[...], (8, 32)).astype(jnp.bfloat16)
+    qall[me, 0] = jnp.full((3, 8, 128), -1.0, jnp.bfloat16)
+    qall[me, 0, 0, :, 0:32] = jnp.broadcast_to(prefix_here[...], (8, 32)).astype(jnp.bfloat16)
     loads[3].wait()
-    for copy in query_sends[:3]:
+    for copy in query_sends[:5]:
         copy.start()
 
     loads[1].wait()
@@ -220,7 +232,7 @@
         return ((z + offset) & 7) * 8
 
     def named_by(d):
-        names = qall[d, 32, 0].astype(jnp.float32)[0:1]
+        names = qall[d, 0, 0].astype(jnp.float32)[0:1]
         return ones_where(names == iota((64, 128), 0).astype(jnp.float32))
 
     before = ones_where(iota((128, 128), 0) < iota((128, 128), 1))
@@ -288,34 +300,28 @@
     pairs(0)
     for way in range(2):
         ring(way, 1, 1).start()
+    hand_on(0, (5, 7))
+    hand_on(1, (8,))
+    pass_on(1, 0)
     pairs(4)
-    pass_on(1, 0)
-    pairs(8)
-    query_sends[0].wait_recv()
-    query_sends[3].start()
-    query_sends[4].start()
-    query_sends[1].wait_recv()
-    query_sends[5].start()
-    query_sends[6].start()
-    pairs(12)
-    loads[6].wait()
-    part = lpart[...] + jnp.dot(pnew[...], nv[...], preferred_element_type=jnp.float32)
-    lpart[...] = part / lsum[...]
-    lmax[...] = lmax[...] + jnp.log2(lsum[...])
+    hand_on(2, (9,))
+    hand_on(3, (6, 10))
 
     def index_at(table, place, last):
         return jnp.minimum(jnp.maximum(index_ref[table * 8, place], 0), last)
 
     def weigh(k):
         for d in range(8):
-            rows = [qall[d, index_at(rank, d * 8 + k, 31)] for rank in range(2)]
+            rows = [qall[d, 1 + index_at(rank, d * 8 + k, 31)] for rank in range(2)]
             both = [row.astype(jnp.float32).reshape(24, 128) for row in rows]
             qpack[k, d] = jnp.concatenate(both, axis=0).astype(jnp.bfloat16)
         scores = dot_t(qpack[k].reshape(384, 128), kvk[offsets[k]])
         top = jnp.max(scores, axis=1, keepdims=True)
         scores = jnp.exp2((scores - top) * to_log2)
-        total = jnp.sum(scores, axis=1, keepdims=True)
         weights[k] = scores.astype(jnp.bfloat16)
+        total = jnp.dot(
+            weights[k], jnp.ones((512, 128), jnp.bfloat16), preferred_element_type=jnp.float32
+        )
         inverse[k] = 1.0 / total
         level = top * to_log2 + jnp.log2(total)
         row = iota((48, 128), 0)
@@ -335,13 +341,10 @@
         for i in range(1, 8):
             part_copy(index, i).start()
 
+    hand_on(5, (11,))
     pass_on(1, 1)
-    query_sends[3].wait_recv()
-    query_sends[7].start()
-    query_sends[5].wait_recv()
-    query_sends[8].start()
-    pass_on(2, 0)
-    for i in (2, 4, 6, 7, 8):
+    hand_on(6, (12,))
+    for i in (4, 7, 8, 11):
         query_sends[i].wait_recv()
     here = ones_where(owners == owner_at(iota((8, 64), 0)) + me)
     match = jnp.concatenate(
@@ -354,6 +357,9 @@
         index_rows[rank * 8 : rank * 8 + 8, 0:64] = dot_t(numbers, chosen).astype(jnp.int32)
     index_copy = pltpu.make_async_copy(index_rows, index_ref, index_sem)
     index_copy.start()
+    pass_on(2, 0)
+    for i in (9, 10, 12):
+        query_sends[i].wait_recv()
     index_copy.wait()
     loads[9].wait()
     loads[10].wait()
@@ -366,6 +372,7 @@
     send_back(0)
     weigh(3)
     weigh(4)
+    pairs(8)
     pass_on(2, 1)
     pl.semaphore_wait(above_here.at[0], 1)
     token(True, 1)
@@ -374,6 +381,7 @@
     blend(3)
     blend(4)
     send_back(1)
+    pairs(12)
     pass_on(3, 0)
     weigh(5)
     weigh(6)
@@ -384,6 +392,10 @@
     blend(5)
     blend(6)
     send_back(2)
+    loads[6].wait()
+    part = lpart[...] + jnp.dot(pnew[...], nv[...], preferred_element_type=jnp.float32)
+    lpart[...] = part / lsum[...]
+    lmax[...] = lmax[...] + jnp.log2(lsum[...])
     ring(0, 4, 0).wait_recv()
     weigh(7)
     for i in range(1, 8):
@@ -435,7 +447,7 @@
         stage[target] = mixed.astype(jnp.bfloat16)
 
     pl.semaphore_wait(above_here.at[2], 1)
-    for batch in ((4, 3, 5, 2), (6, 1, 7, 0)):
+    for batch in ((4, 3), (5, 2), (6, 1), (7, 0)):
         for i in batch:
             combine((head + i) % 8)
         for i in batch:
@@ -502,13 +514,13 @@
             pltpu.VMEM((768, 1), jnp.float32),
             pltpu.VMEM((768, 1), jnp.float32),
             pltpu.VMEM((8, 384, 512), bf16),
-            pltpu.VMEM((8, 384, 1), jnp.float32),
+            pltpu.VMEM((8, 384, 128), jnp.float32),
             pltpu.VMEM((8, 96, 128), bf16),
             dma((11,)),
             dma((2,)),
             dma((2, 4, 2)),
-            dma((9,)),
-            dma((9,)),
+            dma((13,)),
+            dma((13,)),
             dma,
             dma((4,)),
             dma((4,)),

time: 52 us -> 51.4 us (0.988)
  Pallas kernels: 50 us -> 49.2 us
    pallas_call x1, Pallas kernels: 50 us -> 49.2 us  [shards(): pl.pallas_call(kernel, out_shape=jax.ShapeDtypeStruct((8, 96, 128), bf16)...]
where the time goes in v4:
time: 51.4 us; the launch traced here: 50.9 us
  Pallas kernels  49.2 us (96%)
  local copies, waits for them, and re-layouts  1.65 us (3%)
    pallas_call x1, Pallas kernels, shards(): pl.pallas_call(kernel, out_shape=jax.ShapeDtypeStruct((8, 96, 128), bf16)...  49.2 us
    transpose x1, local copies, waits for them, and re-layouts, shards(): ordered = jnp.transpose(gathered.reshape(8, 4, 3, 8, 128), (1, 0, 3, 2, 4))  1.65 us

profile of v4, /device:TPU:1, one launch (start us, length us, event | category | flops | bytes accessed | tf_op | source)
XLA Modules:
  0.0 50.9 jit_solution(7820879965743853378)
XLA Ops:
  0.0 49.2 %shared_prefix.1 = bf16[8,96,128]{2,1,0:T(8,128)(2,1)} custom-call(s32[1,32]{1,0:T(1,128)} %bitcast.31, s32[1,64]{1,0:T(1,128)} %bitcast.32, s32[1,32]{1,0:T(1,128)} %bitcast.33, bf16[32,3,8,128]{3,2,1,0:T(8,128)(2,1)} %bitcast.25, bf16[768,128]{1,0:T(8,128)(2,1)} %bitcast.26, bf16[512,128]{1,0:T(8,128)(2,1)} %bitcast.27, bf16[512,128]{1,0:T(8,128)(2,1)} %bitcast.28, ...), custom_call_target="tpu_custom_call" | custom-call | flops 1200000000 | bytes 3000000 | tf_op jit(solution)/shard_map/shared_prefix/pallas_call | solution.py:487
  49.2 1.7 %copy.13 = bf16[4,8,8,3,128]{4,2,1,3,0:T(8,128)(2,1)} copy(bf16[4,8,8,3,128]{4,2,3,0,1:T(8,128)(2,1)} %bitcast.22) | data formatting | bytes 393216 | tf_op jit(solution)/shard_map/transpose | solution.py:555

commit v5 on v4

--- a/solution.py
+++ b/solution.py
@@ -9,7 +9,8 @@
 
 MESH = pl.DeviceIdType.MESH
 masked_score = -1e30
-offsets = (0, 1, 7, 2, 6, 3, 5, 4)
+offsets = (0, 1, 7, 2, 3, 6, 4, 5)
+hops = (3, 4)
 return_groups = ((0, 3), (3, 2), (5, 2), (7, 1))
 
 
@@ -228,7 +229,9 @@
         return jnp.where(condition, 1.0, 0.0)
 
     def owner_at(k):
-        offset = jnp.where((k & 1) == 1, (k + 1) >> 1, 8 - (k >> 1))
+        offset = jnp.zeros_like(k)
+        for place, value in enumerate(offsets):
+            offset = jnp.where(k == place, value, offset)
         return ((z + offset) & 7) * 8
 
     def named_by(d):
@@ -291,21 +294,27 @@
         for j in range(4):
             pair(first + j)
 
-    def pass_on(hop, which):
-        for way in range(2):
-            ring(way, hop, which).wait_recv()
-            if hop < 3 or which == way:
-                ring(way, hop + 1, which).start()
+    def pass_on(way, hop, which):
+        ring(way, hop, which).wait_recv()
+        if hop < hops[way]:
+            ring(way, hop + 1, which).start()
 
     pairs(0)
     for way in range(2):
         ring(way, 1, 1).start()
+    pairs(4)
     hand_on(0, (5, 7))
     hand_on(1, (8,))
-    pass_on(1, 0)
-    pairs(4)
+    pass_on(1, 1, 0)
+    pass_on(0, 1, 0)
+    pairs(8)
     hand_on(2, (9,))
     hand_on(3, (6, 10))
+    pairs(12)
+    loads[6].wait()
+    part = lpart[...] + jnp.dot(pnew[...], nv[...], preferred_element_type=jnp.float32)
+    lpart[...] = part / lsum[...]
+    lmax[...] = lmax[...] + jnp.log2(lsum[...])
 
     def index_at(table, place, last):
         return jnp.minimum(jnp.maximum(index_ref[table * 8, place], 0), last)
@@ -342,7 +351,8 @@
             part_copy(index, i).start()
 
     hand_on(5, (11,))
-    pass_on(1, 1)
+    pass_on(1, 1, 1)
+    pass_on(0, 1, 1)
     hand_on(6, (12,))
     for i in (4, 7, 8, 11):
         query_sends[i].wait_recv()
@@ -357,7 +367,7 @@
         index_rows[rank * 8 : rank * 8 + 8, 0:64] = dot_t(numbers, chosen).astype(jnp.int32)
     index_copy = pltpu.make_async_copy(index_rows, index_ref, index_sem)
     index_copy.start()
-    pass_on(2, 0)
+    pass_on(1, 2, 0)
     for i in (9, 10, 12):
         query_sends[i].wait_recv()
     index_copy.wait()
@@ -367,40 +377,38 @@
     blend(0)
     weigh(1)
     weigh(2)
+    pass_on(0, 2, 0)
     blend(1)
     blend(2)
     send_back(0)
     weigh(3)
-    weigh(4)
-    pairs(8)
-    pass_on(2, 1)
+    pass_on(1, 2, 1)
+    blend(3)
     pl.semaphore_wait(above_here.at[0], 1)
     token(True, 1)
     pl.semaphore_wait(below_here.at[0], 1)
     token(False, 1)
-    blend(3)
+    pass_on(1, 3, 0)
+    weigh(4)
+    pass_on(0, 2, 1)
+    weigh(5)
+    blend(5)
+    pass_on(1, 3, 1)
     blend(4)
     send_back(1)
-    pairs(12)
-    pass_on(3, 0)
-    weigh(5)
-    weigh(6)
-    pass_on(3, 1)
     pl.semaphore_wait(above_here.at[1], 1)
     token(True, 2)
     pl.semaphore_wait(below_here.at[1], 1)
-    blend(5)
-    blend(6)
-    send_back(2)
-    loads[6].wait()
-    part = lpart[...] + jnp.dot(pnew[...], nv[...], preferred_element_type=jnp.float32)
-    lpart[...] = part / lsum[...]
-    lmax[...] = lmax[...] + jnp.log2(lsum[...])
-    ring(0, 4, 0).wait_recv()
+    pass_on(1, 4, 0)
+    weigh(6)
+    pass_on(0, 3, 0)
     weigh(7)
     for i in range(1, 8):
         stat_copy(i).start()
-    ring(1, 4, 1).wait_recv()
+    pass_on(1, 4, 1)
+    blend(6)
+    send_back(2)
+    pass_on(0, 3, 1)
     blend(7)
     send_back(3)
     for index in range(4):

time: 51.4 us -> 51.9 us (level)
  Pallas kernels: 49.2 us -> 49.9 us
    pallas_call x1, Pallas kernels: 49.2 us -> 49.9 us  [shards(): pl.pallas_call(kernel, out_shape=jax.ShapeDtypeStruct((8, 96, 128), bf16)...]
where the time goes in v5:
time: 51.9 us; the launch traced here: 51.5 us
  Pallas kernels  49.9 us (96%)
  local copies, waits for them, and re-layouts  1.65 us (3%)
    pallas_call x1, Pallas kernels, shards(): pl.pallas_call(kernel, out_shape=jax.ShapeDtypeStruct((8, 96, 128), bf16)...  49.9 us
    transpose x1, local copies, waits for them, and re-layouts, shards(): ordered = jnp.transpose(gathered.reshape(8, 4, 3, 8, 128), (1, 0, 3, 2, 4))  1.65 us

profile of v5, /device:TPU:1, one launch (start us, length us, event | category | flops | bytes accessed | tf_op | source)
XLA Modules:
  0.0 51.5 jit_solution(10671811323938596837)
XLA Ops:
  0.0 49.9 %shared_prefix.1 = bf16[8,96,128]{2,1,0:T(8,128)(2,1)} custom-call(s32[1,32]{1,0:T(1,128)} %bitcast.31, s32[1,64]{1,0:T(1,128)} %bitcast.32, s32[1,32]{1,0:T(1,128)} %bitcast.33, bf16[32,3,8,128]{3,2,1,0:T(8,128)(2,1)} %bitcast.25, bf16[768,128]{1,0:T(8,128)(2,1)} %bitcast.26, bf16[512,128]{1,0:T(8,128)(2,1)} %bitcast.27, bf16[512,128]{1,0:T(8,128)(2,1)} %bitcast.28, ...), custom_call_target="tpu_custom_call" | custom-call | flops 1200000000 | bytes 3000000 | tf_op jit(solution)/shard_map/shared_prefix/pallas_call | solution.py:495
  49.9 1.7 %copy.13 = bf16[4,8,8,3,128]{4,2,1,3,0:T(8,128)(2,1)} copy(bf16[4,8,8,3,128]{4,2,3,0,1:T(8,128)(2,1)} %bitcast.22) | data formatting | bytes 393216 | tf_op jit(solution)/shard_map/transpose | solution.py:563

commit v6 on v4

--- a/solution.py
+++ b/solution.py
@@ -228,7 +228,9 @@
         return jnp.where(condition, 1.0, 0.0)
 
     def owner_at(k):
-        offset = jnp.where((k & 1) == 1, (k + 1) >> 1, 8 - (k >> 1))
+        offset = jnp.zeros_like(k)
+        for place, value in enumerate(offsets):
+            offset = jnp.where(k == place, value, offset)
         return ((z + offset) & 7) * 8
 
     def named_by(d):
@@ -245,6 +247,9 @@
         jnp.ones((8, 64), jnp.float32), mine * earlier
     )
     index_rows[16:24, :] = slots.astype(jnp.int32)
+
+    for way in range(2):
+        ring(way, 1, 1).start()
 
     loads[4].wait()
     loads[5].wait()
@@ -298,14 +303,19 @@
                 ring(way, hop + 1, which).start()
 
     pairs(0)
-    for way in range(2):
-        ring(way, 1, 1).start()
+    pairs(4)
+    pass_on(1, 0)
     hand_on(0, (5, 7))
     hand_on(1, (8,))
-    pass_on(1, 0)
-    pairs(4)
+    pairs(8)
     hand_on(2, (9,))
     hand_on(3, (6, 10))
+    pass_on(1, 1)
+    pairs(12)
+    loads[6].wait()
+    part = lpart[...] + jnp.dot(pnew[...], nv[...], preferred_element_type=jnp.float32)
+    lpart[...] = part / lsum[...]
+    lmax[...] = lmax[...] + jnp.log2(lsum[...])
 
     def index_at(table, place, last):
         return jnp.minimum(jnp.maximum(index_ref[table * 8, place], 0), last)
@@ -342,8 +352,8 @@
             part_copy(index, i).start()
 
     hand_on(5, (11,))
-    pass_on(1, 1)
     hand_on(6, (12,))
+    pass_on(2, 0)
     for i in (4, 7, 8, 11):
         query_sends[i].wait_recv()
     here = ones_where(owners == owner_at(iota((8, 64), 0)) + me)
@@ -357,7 +367,6 @@
         index_rows[rank * 8 : rank * 8 + 8, 0:64] = dot_t(numbers, chosen).astype(jnp.int32)
     index_copy = pltpu.make_async_copy(index_rows, index_ref, index_sem)
     index_copy.start()
-    pass_on(2, 0)
     for i in (9, 10, 12):
         query_sends[i].wait_recv()
     index_copy.wait()
@@ -365,37 +374,31 @@
     loads[10].wait()
     weigh(0)
     blend(0)
+    pass_on(2, 1)
     weigh(1)
+    blend(1)
     weigh(2)
-    blend(1)
     blend(2)
     send_back(0)
-    weigh(3)
-    weigh(4)
-    pairs(8)
-    pass_on(2, 1)
+    pass_on(3, 0)
     pl.semaphore_wait(above_here.at[0], 1)
     token(True, 1)
     pl.semaphore_wait(below_here.at[0], 1)
     token(False, 1)
+    weigh(3)
+    weigh(4)
     blend(3)
     blend(4)
     send_back(1)
-    pairs(12)
-    pass_on(3, 0)
-    weigh(5)
-    weigh(6)
     pass_on(3, 1)
     pl.semaphore_wait(above_here.at[1], 1)
     token(True, 2)
     pl.semaphore_wait(below_here.at[1], 1)
+    weigh(5)
+    weigh(6)
     blend(5)
     blend(6)
     send_back(2)
-    loads[6].wait()
-    part = lpart[...] + jnp.dot(pnew[...], nv[...], preferred_element_type=jnp.float32)
-    lpart[...] = part / lsum[...]
-    lmax[...] = lmax[...] + jnp.log2(lsum[...])
     ring(0, 4, 0).wait_recv()
     weigh(7)
     for i in range(1, 8):

time: 51.4 us -> 50.8 us (0.988)
  Pallas kernels: 49.2 us -> 48.6 us
    pallas_call x1, Pallas kernels: 49.2 us -> 48.6 us  [shards(): pl.pallas_call(kernel, out_shape=jax.ShapeDtypeStruct((8, 96, 128), bf16)...]
where the time goes in v6:
time: 50.8 us; the launch traced here: 50.3 us
  Pallas kernels  48.6 us (96%)
  local copies, waits for them, and re-layouts  1.65 us (3%)
    pallas_call x1, Pallas kernels, shards(): pl.pallas_call(kernel, out_shape=jax.ShapeDtypeStruct((8, 96, 128), bf16)...  48.6 us
    transpose x1, local copies, waits for them, and re-layouts, shards(): ordered = jnp.transpose(gathered.reshape(8, 4, 3, 8, 128), (1, 0, 3, 2, 4))  1.65 us

profile of v6, /device:TPU:1, one launch (start us, length us, event | category | flops | bytes accessed | tf_op | source)
XLA Modules:
  0.0 50.3 jit_solution(5529433372659825660)
XLA Ops:
  0.0 48.6 %shared_prefix.1 = bf16[8,96,128]{2,1,0:T(8,128)(2,1)} custom-call(s32[1,32]{1,0:T(1,128)} %bitcast.31, s32[1,64]{1,0:T(1,128)} %bitcast.32, s32[1,32]{1,0:T(1,128)} %bitcast.33, bf16[32,3,8,128]{3,2,1,0:T(8,128)(2,1)} %bitcast.25, bf16[768,128]{1,0:T(8,128)(2,1)} %bitcast.26, bf16[512,128]{1,0:T(8,128)(2,1)} %bitcast.27, bf16[512,128]{1,0:T(8,128)(2,1)} %bitcast.28, ...), custom_call_target="tpu_custom_call" | custom-call | flops 1200000000 | bytes 3000000 | tf_op jit(solution)/shard_map/shared_prefix/pallas_call | solution.py:490
  48.7 1.7 %copy.13 = bf16[4,8,8,3,128]{4,2,1,3,0:T(8,128)(2,1)} copy(bf16[4,8,8,3,128]{4,2,3,0,1:T(8,128)(2,1)} %bitcast.22) | data formatting | bytes 393216 | tf_op jit(solution)/shard_map/transpose | solution.py:558

commit v7 on v6

--- a/solution.py
+++ b/solution.py
@@ -52,6 +52,7 @@
     pnew,
     lpart,
     lmax,
+    share,
     lsum,
     weights,
     inverse,
@@ -406,10 +407,6 @@
     ring(1, 4, 1).wait_recv()
     blend(7)
     send_back(3)
-    for index in range(4):
-        wait_for(orecv.at[pl.ds(*return_groups[index]), seven], o_recv_sem.at[index])
-    wait_for(srecv.at[:, seven], s_recv_sem)
-
     def head_copy(i):
         peer = (head + i) % 8
         return pltpu.make_async_remote_copy(
@@ -421,34 +418,44 @@
             device_id_type=MESH,
         )
 
-    def combine(target):
-        parts = []
+    def settle(target):
         levels = []
-        row = lax.broadcasted_iota(jnp.int32, (24, 128), 0)
-        lane = lax.broadcasted_iota(jnp.int32, (24, 128), 1)
+        row = iota((24, 128), 0)
+        lane = iota((24, 128), 1)
         for j in range(4):
             slot = index_at(2, target * 4 + j, 127)
-            which = slot % 2
-            both = orecv[slot // 16, (slot // 2) % 8].astype(jnp.float32)
             stats = srecv[slot // 16, (slot // 2) % 8]
-            parts.append(jnp.where(row * 0 + which == 0, both[:24], both[24:]))
             levels.append(
                 jnp.sum(
-                    jnp.where(lane == row + 24 * which, stats, 0.0), axis=1, keepdims=True
+                    jnp.where(lane == row + 24 * (slot % 2), stats, 0.0), axis=1, keepdims=True
                 )
             )
-        parts = jnp.concatenate(parts, axis=0)
         levels = jnp.concatenate(levels, axis=0)
-        rows = pl.ds(pl.multiple_of(target * 96, 96), 96)
+        rows = pl.ds(target * 96, 96)
         local = lmax[rows, :]
         top = jnp.maximum(levels, local)
         pre_factor = jnp.exp2(levels - top)
         local_factor = jnp.exp2(local - top)
-        mixed = (parts * pre_factor + lpart[rows, :] * local_factor) / (
-            pre_factor + local_factor
-        )
+        inverse_sum = 1.0 / (pre_factor + local_factor)
+        share[rows, :] = pre_factor * inverse_sum
+        lpart[rows, :] = lpart[rows, :] * (local_factor * inverse_sum)
+
+    def combine(target):
+        parts = []
+        row = iota((24, 128), 0)
+        for j in range(4):
+            slot = index_at(2, target * 4 + j, 127)
+            both = orecv[slot // 16, (slot // 2) % 8].astype(jnp.float32)
+            parts.append(jnp.where(row * 0 + slot % 2 == 0, both[:24], both[24:]))
+        rows = pl.ds(pl.multiple_of(target * 96, 96), 96)
+        mixed = jnp.concatenate(parts, axis=0) * share[rows, :] + lpart[rows, :]
         stage[target] = mixed.astype(jnp.bfloat16)
 
+    wait_for(srecv.at[:, seven], s_recv_sem)
+    for target in range(8):
+        settle(target)
+    for index in range(4):
+        wait_for(orecv.at[pl.ds(*return_groups[index]), seven], o_recv_sem.at[index])
     pl.semaphore_wait(above_here.at[2], 1)
     for batch in ((4, 3), (5, 2), (6, 1), (7, 0)):
         for i in batch:
@@ -516,6 +523,7 @@
             pltpu.VMEM((768, 128), jnp.float32),
             pltpu.VMEM((768, 1), jnp.float32),
             pltpu.VMEM((768, 1), jnp.float32),
+            pltpu.VMEM((768, 1), jnp.float32),
             pltpu.VMEM((8, 384, 512), bf16),
             pltpu.VMEM((8, 384, 128), jnp.float32),
             pltpu.VMEM((8, 96, 128), bf16),

time: 50.8 us -> 50.5 us (level)
  no operation moved by 1% of the time
where the time goes in v7:
time: 50.5 us; the launch traced here: 50.1 us
  Pallas kernels  48.5 us (96%)
  local copies, waits for them, and re-layouts  1.65 us (3%)
    pallas_call x1, Pallas kernels, shards(): pl.pallas_call(kernel, out_shape=jax.ShapeDtypeStruct((8, 96, 128), bf16)...  48.5 us
    transpose x1, local copies, waits for them, and re-layouts, shards(): ordered = jnp.transpose(gathered.reshape(8, 4, 3, 8, 128), (1, 0, 3, 2, 4))  1.65 us

profile of v7, /device:TPU:1, one launch (start us, length us, event | category | flops | bytes accessed | tf_op | source)
XLA Modules:
  0.0 50.1 jit_solution(18440507178618646931)
XLA Ops:
  0.0 48.5 %shared_prefix.1 = bf16[8,96,128]{2,1,0:T(8,128)(2,1)} custom-call(s32[1,32]{1,0:T(1,128)} %bitcast.31, s32[1,64]{1,0:T(1,128)} %bitcast.32, s32[1,32]{1,0:T(1,128)} %bitcast.33, bf16[32,3,8,128]{3,2,1,0:T(8,128)(2,1)} %bitcast.25, bf16[768,128]{1,0:T(8,128)(2,1)} %bitcast.26, bf16[512,128]{1,0:T(8,128)(2,1)} %bitcast.27, bf16[512,128]{1,0:T(8,128)(2,1)} %bitcast.28, ...), custom_call_target="tpu_custom_call" | custom-call | flops 1200000000 | bytes 3000000 | tf_op jit(solution)/shard_map/shared_prefix/pallas_call | solution.py:497
  48.5 1.7 %copy.13 = bf16[4,8,8,3,128]{4,2,1,3,0:T(8,128)(2,1)} copy(bf16[4,8,8,3,128]{4,2,3,0,1:T(8,128)(2,1)} %bitcast.22) | data formatting | bytes 393216 | tf_op jit(solution)/shard_map/transpose | solution.py:566

commit v8 on v7

--- a/solution.py
+++ b/solution.py
@@ -10,7 +10,7 @@
 MESH = pl.DeviceIdType.MESH
 masked_score = -1e30
 offsets = (0, 1, 7, 2, 6, 3, 5, 4)
-return_groups = ((0, 3), (3, 2), (5, 2), (7, 1))
+return_groups = ((0, 3), (3, 2), (5, 2))
 
 
 def dot_t(a, b):
@@ -72,6 +72,12 @@
     own_sem,
     above_here,
     below_here,
+    far_q_send_sem,
+    far_q_recv_sem,
+    far_o_send_sem,
+    far_o_recv_sem,
+    far_s_send_sem,
+    far_s_recv_sem,
 ):
     pre = lax.axis_index("pre")
     head = lax.axis_index("head")
@@ -170,7 +176,27 @@
         return plane_copy(osend, orecv, blocks, o_send_sem.at[index], o_recv_sem.at[index], i)
 
     def stat_copy(i):
-        return plane_copy(ssend, srecv, pl.ds(0, 8), s_send_sem, s_recv_sem, i)
+        return plane_copy(ssend, srecv, seven, s_send_sem, s_recv_sem, i)
+
+    def far_query(way):
+        return pltpu.make_async_remote_copy(
+            src_ref=qpack.at[7, pl.ds(4 * way, 4)],
+            dst_ref=qpack.at[5 + way, pl.ds(8, 4)],
+            send_sem=far_q_send_sem.at[way],
+            recv_sem=far_q_recv_sem.at[way],
+            device_id=((right, left)[way], head),
+            device_id_type=MESH,
+        )
+
+    def far_copy(source, target, send_sem, recv_sem, d):
+        return pltpu.make_async_remote_copy(
+            src_ref=source.at[7, d],
+            dst_ref=target.at[7, me],
+            send_sem=send_sem,
+            recv_sem=recv_sem,
+            device_id=((left if d < 4 else right) - me + d, head),
+            device_id_type=MESH,
+        )
 
     pl.semaphore_wait(barrier, 7)
     for way in range(2):
@@ -300,7 +326,7 @@
     def pass_on(hop, which):
         for way in range(2):
             ring(way, hop, which).wait_recv()
-            if hop < 3 or which == way:
+            if hop < 3:
                 ring(way, hop + 1, which).start()
 
     pairs(0)
@@ -321,31 +347,47 @@
     def index_at(table, place, last):
         return jnp.minimum(jnp.maximum(index_ref[table * 8, place], 0), last)
 
-    def weigh(k):
+    def pack(k):
         for d in range(8):
             rows = [qall[d, 1 + index_at(rank, d * 8 + k, 31)] for rank in range(2)]
             both = [row.astype(jnp.float32).reshape(24, 128) for row in rows]
             qpack[k, d] = jnp.concatenate(both, axis=0).astype(jnp.bfloat16)
-        scores = dot_t(qpack[k].reshape(384, 128), kvk[offsets[k]])
+
+    def sources(k):
+        return 12 if k in (5, 6) else 8
+
+    def weigh(k):
+        pack(k)
+        count = sources(k)
+        scores = dot_t(qpack[k, 0:count].reshape(count * 48, 128), kvk[offsets[k]])
         top = jnp.max(scores, axis=1, keepdims=True)
         scores = jnp.exp2((scores - top) * to_log2)
-        weights[k] = scores.astype(jnp.bfloat16)
+        weights[k, 0 : count * 48] = scores.astype(jnp.bfloat16)
         total = jnp.dot(
-            weights[k], jnp.ones((512, 128), jnp.bfloat16), preferred_element_type=jnp.float32
-        )
-        inverse[k] = 1.0 / total
+            weights[k, 0 : count * 48],
+            jnp.ones((512, 128), jnp.bfloat16),
+            preferred_element_type=jnp.float32,
+        )
+        inverse[k, 0 : count * 48] = 1.0 / total
         level = top * to_log2 + jnp.log2(total)
         row = iota((48, 128), 0)
         lane = iota((48, 128), 1)
-        for d in range(8):
-            ssend[k, d] = jnp.sum(
+        for d in range(count):
+            block, place = (k, d) if d < 8 else (7, d - 8 + 4 * (k - 5))
+            ssend[block, place] = jnp.sum(
                 jnp.where(row == lane, level[d * 48 : d * 48 + 48], 0.0), axis=0, keepdims=True
             )
         srecv[k, me] = ssend[k, me]
 
     def blend(k):
-        part = jnp.dot(weights[k], kvv[offsets[k]], preferred_element_type=jnp.float32)
-        osend[k] = (part * inverse[k]).astype(jnp.bfloat16).reshape(8, 48, 128)
+        count = sources(k)
+        part = jnp.dot(
+            weights[k, 0 : count * 48], kvv[offsets[k]], preferred_element_type=jnp.float32
+        )
+        part = (part * inverse[k, 0 : count * 48]).astype(jnp.bfloat16).reshape(count, 48, 128)
+        osend[k] = part[0:8]
+        if count > 8:
+            osend[7, 4 * (k - 5) : 4 * (k - 5) + 4] = part[8:12]
         orecv[k, me] = osend[k, me]
 
     def send_back(index):
@@ -373,6 +415,9 @@
     index_copy.wait()
     loads[9].wait()
     loads[10].wait()
+    pack(7)
+    for way in range(2):
+        far_query(way).start()
     weigh(0)
     blend(0)
     pass_on(2, 1)
@@ -391,22 +436,24 @@
     blend(3)
     blend(4)
     send_back(1)
-    pass_on(3, 1)
+    for way in range(2):
+        far_query(way).wait_recv()
+    weigh(5)
+    weigh(6)
+    for d in range(8):
+        far_copy(ssend, srecv, far_s_send_sem, far_s_recv_sem, d).start()
+    for i in range(1, 8):
+        stat_copy(i).start()
     pl.semaphore_wait(above_here.at[1], 1)
     token(True, 2)
     pl.semaphore_wait(below_here.at[1], 1)
-    weigh(5)
-    weigh(6)
-    blend(5)
-    blend(6)
+    pass_on(3, 1)
+    for k in (5, 6):
+        blend(k)
+        for d in range(4 * (k - 5), 4 * (k - 5) + 4):
+            far_copy(osend, orecv, far_o_send_sem, far_o_recv_sem, d).start()
     send_back(2)
-    ring(0, 4, 0).wait_recv()
-    weigh(7)
-    for i in range(1, 8):
-        stat_copy(i).start()
-    ring(1, 4, 1).wait_recv()
-    blend(7)
-    send_back(3)
+
     def head_copy(i):
         peer = (head + i) % 8
         return pltpu.make_async_remote_copy(
@@ -451,11 +498,13 @@
         mixed = jnp.concatenate(parts, axis=0) * share[rows, :] + lpart[rows, :]
         stage[target] = mixed.astype(jnp.bfloat16)
 
-    wait_for(srecv.at[:, seven], s_recv_sem)
+    wait_for(srecv.at[seven, seven], s_recv_sem)
+    wait_for(srecv.at[7], far_s_recv_sem)
     for target in range(8):
         settle(target)
-    for index in range(4):
+    for index in range(3):
         wait_for(orecv.at[pl.ds(*return_groups[index]), seven], o_recv_sem.at[index])
+    wait_for(orecv.at[7], far_o_recv_sem)
     pl.semaphore_wait(above_here.at[2], 1)
     for batch in ((4, 3), (5, 2), (6, 1), (7, 0)):
         for i in batch:
@@ -467,12 +516,16 @@
     own.start()
 
     for which in range(2):
-        wait_for((kvk, kvv)[which].at[seven], ring_send.at[which])
+        wait_for((kvk, kvv)[which].at[pl.ds(0, 6)], ring_send.at[which])
     for copy in query_sends:
         copy.wait_send()
-    for index in range(4):
+    for index in range(3):
         wait_for(osend.at[pl.ds(*return_groups[index]), seven], o_send_sem.at[index])
-    wait_for(ssend.at[:, seven], s_send_sem)
+    wait_for(ssend.at[seven, seven], s_send_sem)
+    for way in range(2):
+        far_query(way).wait_send()
+    wait_for(osend.at[7], far_o_send_sem)
+    wait_for(ssend.at[7], far_s_send_sem)
     wait_for(stage.at[seven], y_send_sem)
     own.wait()
     wait_for(out_ref.at[seven], y_recv_sem)
@@ -513,7 +566,7 @@
             pltpu.VMEM((3072, 128), bf16),
             pltpu.VMEM((96, 128), bf16),
             pltpu.VMEM((96, 128), bf16),
-            pltpu.VMEM((8, 8, 48, 128), bf16),
+            pltpu.VMEM((8, 12, 48, 128), bf16),
             pltpu.VMEM((8, 8, 48, 128), bf16),
             pltpu.VMEM((8, 8, 48, 128), bf16),
             pltpu.VMEM((8, 8, 1, 128), jnp.float32),
@@ -524,8 +577,8 @@
             pltpu.VMEM((768, 1), jnp.float32),
             pltpu.VMEM((768, 1), jnp.float32),
             pltpu.VMEM((768, 1), jnp.float32),
-            pltpu.VMEM((8, 384, 512), bf16),
-            pltpu.VMEM((8, 384, 128), jnp.float32),
+            pltpu.VMEM((8, 576, 512), bf16),
+            pltpu.VMEM((8, 576, 128), jnp.float32),
             pltpu.VMEM((8, 96, 128), bf16),
             dma((11,)),
             dma((2,)),
@@ -542,6 +595,12 @@
             dma,
             pltpu.SemaphoreType.REGULAR((3,)),
             pltpu.SemaphoreType.REGULAR((2,)),
+            dma((2,)),
+            dma((2,)),
+            dma,
+            dma,
+            dma,
+            dma,
         ],
         compiler_params=pltpu.CompilerParams(
             collective_id=0, has_side_effects=True, vmem_limit_bytes=60 * 1024 * 1024

time: 50.5 us -> 48.6 us (0.962)
  Pallas kernels: 48.5 us -> 46.8 us
    pallas_call x1, Pallas kernels: 48.5 us -> 46.8 us  [shards(): pl.pallas_call(kernel, out_shape=jax.ShapeDtypeStruct((8, 96, 128), bf16)...]
where the time goes in v8:
time: 48.6 us; the launch traced here: 48.4 us
  Pallas kernels  46.8 us (96%)
  local copies, waits for them, and re-layouts  1.65 us (3%)
    pallas_call x1, Pallas kernels, shards(): pl.pallas_call(kernel, out_shape=jax.ShapeDtypeStruct((8, 96, 128), bf16)...  46.8 us
    transpose x1, local copies, waits for them, and re-layouts, shards(): ordered = jnp.transpose(gathered.reshape(8, 4, 3, 8, 128), (1, 0, 3, 2, 4))  1.65 us

profile of v8, /device:TPU:1, one launch (start us, length us, event | category | flops | bytes accessed | tf_op | source)
XLA Modules:
  0.0 48.4 jit_solution(13538506591283482715)
XLA Ops:
  0.0 46.8 %shared_prefix.1 = bf16[8,96,128]{2,1,0:T(8,128)(2,1)} custom-call(s32[1,32]{1,0:T(1,128)} %bitcast.31, s32[1,64]{1,0:T(1,128)} %bitcast.32, s32[1,32]{1,0:T(1,128)} %bitcast.33, bf16[32,3,8,128]{3,2,1,0:T(8,128)(2,1)} %bitcast.25, bf16[768,128]{1,0:T(8,128)(2,1)} %bitcast.26, bf16[512,128]{1,0:T(8,128)(2,1)} %bitcast.27, bf16[512,128]{1,0:T(8,128)(2,1)} %bitcast.28, ...), custom_call_target="tpu_custom_call" | custom-call | flops 1200000000 | bytes 3000000 | tf_op jit(solution)/shard_map/shared_prefix/pallas_call | solution.py:550
  46.8 1.7 %copy.13 = bf16[4,8,8,3,128]{4,2,1,3,0:T(8,128)(2,1)} copy(bf16[4,8,8,3,128]{4,2,3,0,1:T(8,128)(2,1)} %bitcast.22) | data formatting | bytes 393216 | tf_op jit(solution)/shard_map/transpose | solution.py:625

commit v9 on v8

--- a/solution.py
+++ b/solution.py
@@ -324,7 +324,7 @@
             pair(first + j)
 
     def pass_on(hop, which):
-        for way in range(2):
+        for way in (1, 0):
             ring(way, hop, which).wait_recv()
             if hop < 3:
                 ring(way, hop + 1, which).start()
@@ -447,8 +447,8 @@
     pl.semaphore_wait(above_here.at[1], 1)
     token(True, 2)
     pl.semaphore_wait(below_here.at[1], 1)
-    pass_on(3, 1)
     for k in (5, 6):
+        ring(6 - k, 3, 1).wait_recv()
         blend(k)
         for d in range(4 * (k - 5), 4 * (k - 5) + 4):
             far_copy(osend, orecv, far_o_send_sem, far_o_recv_sem, d).start()
@@ -549,9 +549,9 @@
     dma = pltpu.SemaphoreType.DMA
     gathered = pl.pallas_call(
         kernel,
-        out_shape=jax.ShapeDtypeStruct((8, 96, 128), bf16),
+        out_shape=pltpu.VMEM((8, 96, 128), bf16),
         in_specs=[anywhere] * 11,
-        out_specs=anywhere,
+        out_specs=pl.BlockSpec(memory_space=pltpu.VMEM),
         scratch_shapes=[
             pltpu.VMEM((1, 32), jnp.int32),
             pltpu.VMEM((1, 64), jnp.int32),

time: 48.6 us -> 47.3 us (0.973)
  local copies, waits for them, and re-layouts: 1.65 us -> 0.72 us
    transpose x1, local copies, waits for them, and re-layouts: 1.65 us -> 0.72 us  [shards(): ordered = jnp.transpose(gathered.reshape(8, 4, 3, 8, 128), (1, 0, 3, 2, 4))]
where the time goes in v9:
time: 47.3 us; the launch traced here: 47.2 us
  Pallas kernels  46.4 us (98%)
  local copies, waits for them, and re-layouts  0.72 us (2%)
    pallas_call x1, Pallas kernels, shards(): pl.pallas_call(kernel, out_shape=pltpu.VMEM((8, 96, 128), bf16), in_specs...  46.4 us

profile of v9, /device:TPU:1, one launch (start us, length us, event | category | flops | bytes accessed | tf_op | source)
XLA Modules:
  0.0 47.2 jit_solution(10747796894984344452)
XLA Ops:
  0.0 46.4 %shared_prefix.1 = bf16[8,96,128]{2,1,0:T(8,128)(2,1)S(1)} custom-call(s32[1,32]{1,0:T(1,128)} %bitcast.31, s32[1,64]{1,0:T(1,128)} %bitcast.32, s32[1,32]{1,0:T(1,128)} %bitcast.33, bf16[32,3,8,128]{3,2,1,0:T(8,128)(2,1)} %bitcast.25, bf16[768,128]{1,0:T(8,128)(2,1)} %bitcast.26, bf16[512,128]{1,0:T(8,128)(2,1)} %bitcast.27, bf16[512,128]{1,0:T(8,128)(2,1)} %bitcast.28, ...), custom_call_target="tpu_custom_call" | custom-call | flops 1200000000 | bytes 3000000 | tf_op jit(solution)/shard_map/shared_prefix/pallas_call | solution.py:550
  46.4 0.7 %copy.13 = bf16[4,8,8,3,128]{4,2,1,3,0:T(8,128)(2,1)} copy(bf16[4,8,8,3,128]{4,2,3,0,1:T(8,128)(2,1)S(1)} %bitcast.22) | data formatting | bytes 393216 | tf_op jit(solution)/shard_map/transpose | solution.py:625

commit v10 on v9

--- a/solution.py
+++ b/solution.py
@@ -9,7 +9,7 @@
 
 MESH = pl.DeviceIdType.MESH
 masked_score = -1e30
-offsets = (0, 1, 7, 2, 6, 3, 5, 4)
+offsets = (0, 7, 1, 6, 2, 5, 3, 4)
 return_groups = ((0, 3), (3, 2), (5, 2))
 
 
@@ -101,7 +101,7 @@
         )
 
     above, below = (head + 1) % 8, (head + 7) % 8
-    for peer in (right, left, plane + ahead, plane + behind, plane + sibling):
+    for peer in (left, plane + ahead, plane + behind, plane + sibling):
         greet(peer, head)
     greet(pre, above)
     greet(pre, below)
@@ -181,7 +181,7 @@
     def far_query(way):
         return pltpu.make_async_remote_copy(
             src_ref=qpack.at[7, pl.ds(4 * way, 4)],
-            dst_ref=qpack.at[5 + way, pl.ds(8, 4)],
+            dst_ref=qpack.at[6 - way, pl.ds(8, 4)],
             send_sem=far_q_send_sem.at[way],
             recv_sem=far_q_recv_sem.at[way],
             device_id=((right, left)[way], head),
@@ -198,9 +198,8 @@
             device_id_type=MESH,
         )
 
-    pl.semaphore_wait(barrier, 7)
-    for way in range(2):
-        ring(way, 1, 0).start()
+    pl.semaphore_wait(barrier, 6)
+    ring(0, 1, 0).start()
     for i in (4, 5, 2, 7, 8, 6, 9, 10):
         loads[i].start()
 
@@ -255,9 +254,7 @@
         return jnp.where(condition, 1.0, 0.0)
 
     def owner_at(k):
-        offset = jnp.zeros_like(k)
-        for place, value in enumerate(offsets):
-            offset = jnp.where(k == place, value, offset)
+        offset = jnp.where((k & 1) == 1, 8 - ((k + 1) >> 1), k >> 1)
         return ((z + offset) & 7) * 8
 
     def named_by(d):
@@ -275,8 +272,7 @@
     )
     index_rows[16:24, :] = slots.astype(jnp.int32)
 
-    for way in range(2):
-        ring(way, 1, 1).start()
+    ring(0, 1, 1).start()
 
     loads[4].wait()
     loads[5].wait()
@@ -323,21 +319,22 @@
         for j in range(4):
             pair(first + j)
 
-    def pass_on(hop, which):
-        for way in (1, 0):
-            ring(way, hop, which).wait_recv()
-            if hop < 3:
-                ring(way, hop + 1, which).start()
+    def pass_on(way, hop, which):
+        ring(way, hop, which).wait_recv()
+        if hop < 3:
+            ring(way, hop + 1, which).start()
 
     pairs(0)
     pairs(4)
-    pass_on(1, 0)
+    pass_on(0, 1, 0)
+    ring(1, 1, 0).start()
     hand_on(0, (5, 7))
     hand_on(1, (8,))
     pairs(8)
     hand_on(2, (9,))
     hand_on(3, (6, 10))
-    pass_on(1, 1)
+    ring(1, 1, 1).start()
+    pass_on(0, 1, 1)
     pairs(12)
     loads[6].wait()
     part = lpart[...] + jnp.dot(pnew[...], nv[...], preferred_element_type=jnp.float32)
@@ -373,7 +370,7 @@
         row = iota((48, 128), 0)
         lane = iota((48, 128), 1)
         for d in range(count):
-            block, place = (k, d) if d < 8 else (7, d - 8 + 4 * (k - 5))
+            block, place = (k, d) if d < 8 else (7, d - 8 + 4 * (6 - k))
             ssend[block, place] = jnp.sum(
                 jnp.where(row == lane, level[d * 48 : d * 48 + 48], 0.0), axis=0, keepdims=True
             )
@@ -387,7 +384,7 @@
         part = (part * inverse[k, 0 : count * 48]).astype(jnp.bfloat16).reshape(count, 48, 128)
         osend[k] = part[0:8]
         if count > 8:
-            osend[7, 4 * (k - 5) : 4 * (k - 5) + 4] = part[8:12]
+            osend[7, 4 * (6 - k) : 4 * (6 - k) + 4] = part[8:12]
         orecv[k, me] = osend[k, me]
 
     def send_back(index):
@@ -396,7 +393,8 @@
 
     hand_on(5, (11,))
     hand_on(6, (12,))
-    pass_on(2, 0)
+    pass_on(1, 1, 0)
+    pass_on(0, 2, 0)
     for i in (4, 7, 8, 11):
         query_sends[i].wait_recv()
     here = ones_where(owners == owner_at(iota((8, 64), 0)) + me)
@@ -420,25 +418,37 @@
         far_query(way).start()
     weigh(0)
     blend(0)
-    pass_on(2, 1)
+    pass_on(1, 1, 1)
+    pass_on(0, 2, 1)
     weigh(1)
     blend(1)
     weigh(2)
     blend(2)
     send_back(0)
-    pass_on(3, 0)
+    pass_on(1, 2, 0)
+    pass_on(0, 3, 0)
     pl.semaphore_wait(above_here.at[0], 1)
     token(True, 1)
     pl.semaphore_wait(below_here.at[0], 1)
     token(False, 1)
     weigh(3)
+    blend(3)
     weigh(4)
-    blend(3)
+    pass_on(1, 2, 1)
+    pass_on(0, 3, 1)
     blend(4)
     send_back(1)
+
+    def far_back(k):
+        for d in range(4 * (6 - k), 4 * (6 - k) + 4):
+            far_copy(osend, orecv, far_o_send_sem, far_o_recv_sem, d).start()
+
     for way in range(2):
         far_query(way).wait_recv()
     weigh(5)
+    blend(5)
+    far_back(5)
+    pass_on(1, 3, 0)
     weigh(6)
     for d in range(8):
         far_copy(ssend, srecv, far_s_send_sem, far_s_recv_sem, d).start()
@@ -447,11 +457,9 @@
     pl.semaphore_wait(above_here.at[1], 1)
     token(True, 2)
     pl.semaphore_wait(below_here.at[1], 1)
-    for k in (5, 6):
-        ring(6 - k, 3, 1).wait_recv()
-        blend(k)
-        for d in range(4 * (k - 5), 4 * (k - 5) + 4):
-            far_copy(osend, orecv, far_o_send_sem, far_o_recv_sem, d).start()
+    pass_on(1, 3, 1)
+    blend(6)
+    far_back(6)
     send_back(2)
 
     def head_copy(i):

time: 47.3 us -> 49.4 us (1.044)
  Pallas kernels: 46.4 us -> 48.3 us
    pallas_call x1, Pallas kernels: 46.4 us -> 48.3 us  [shards(): pl.pallas_call(kernel, out_shape=pltpu.VMEM((8, 96, 128), bf16), in_specs...]
where the time goes in v10:
time: 49.4 us; the launch traced here: 49 us
  Pallas kernels  48.3 us (98%)
  local copies, waits for them, and re-layouts  0.72 us (1%)
    pallas_call x1, Pallas kernels, shards(): pl.pallas_call(kernel, out_shape=pltpu.VMEM((8, 96, 128), bf16), in_specs...  48.3 us

profile of v10, /device:TPU:1, one launch (start us, length us, event | category | flops | bytes accessed | tf_op | source)
XLA Modules:
  0.0 49.0 jit_solution(16463669191885972167)
XLA Ops:
  0.0 48.3 %shared_prefix.1 = bf16[8,96,128]{2,1,0:T(8,128)(2,1)S(1)} custom-call(s32[1,32]{1,0:T(1,128)} %bitcast.31, s32[1,64]{1,0:T(1,128)} %bitcast.32, s32[1,32]{1,0:T(1,128)} %bitcast.33, bf16[32,3,8,128]{3,2,1,0:T(8,128)(2,1)} %bitcast.25, bf16[768,128]{1,0:T(8,128)(2,1)} %bitcast.26, bf16[512,128]{1,0:T(8,128)(2,1)} %bitcast.27, bf16[512,128]{1,0:T(8,128)(2,1)} %bitcast.28, ...), custom_call_target="tpu_custom_call" | custom-call | flops 1200000000 | bytes 3000000 | tf_op jit(solution)/shard_map/shared_prefix/pallas_call | solution.py:558
  48.3 0.7 %copy.13 = bf16[4,8,8,3,128]{4,2,1,3,0:T(8,128)(2,1)} copy(bf16[4,8,8,3,128]{4,2,3,0,1:T(8,128)(2,1)S(1)} %bitcast.22) | data formatting | bytes 393216 | tf_op jit(solution)/shard_map/transpose | solution.py:633

commit v11 on v9

--- a/solution.py
+++ b/solution.py
@@ -10,7 +10,7 @@
 MESH = pl.DeviceIdType.MESH
 masked_score = -1e30
 offsets = (0, 1, 7, 2, 6, 3, 5, 4)
-return_groups = ((0, 3), (3, 2), (5, 2))
+return_groups = ((0, 3), (3, 2), (5, 1), (6, 1))
 
 
 def dot_t(a, b):
@@ -452,7 +452,7 @@
         blend(k)
         for d in range(4 * (k - 5), 4 * (k - 5) + 4):
             far_copy(osend, orecv, far_o_send_sem, far_o_recv_sem, d).start()
-    send_back(2)
+        send_back(k - 3)
 
     def head_copy(i):
         peer = (head + i) % 8
@@ -502,7 +502,7 @@
     wait_for(srecv.at[7], far_s_recv_sem)
     for target in range(8):
         settle(target)
-    for index in range(3):
+    for index in range(4):
         wait_for(orecv.at[pl.ds(*return_groups[index]), seven], o_recv_sem.at[index])
     wait_for(orecv.at[7], far_o_recv_sem)
     pl.semaphore_wait(above_here.at[2], 1)
@@ -519,7 +519,7 @@
         wait_for((kvk, kvv)[which].at[pl.ds(0, 6)], ring_send.at[which])
     for copy in query_sends:
         copy.wait_send()
-    for index in range(3):
+    for index in range(4):
         wait_for(osend.at[pl.ds(*return_groups[index]), seven], o_send_sem.at[index])
     wait_for(ssend.at[seven, seven], s_send_sem)
     for way in range(2):

time: 47.3 us -> 47.4 us (level)
  no operation moved by 1% of the time
where the time goes in v11:
time: 47.4 us; the launch traced here: 47 us
  Pallas kernels  46.3 us (98%)
  local copies, waits for them, and re-layouts  0.72 us (2%)
    pallas_call x1, Pallas kernels, shards(): pl.pallas_call(kernel, out_shape=pltpu.VMEM((8, 96, 128), bf16), in_specs...  46.3 us

profile of v11, /device:TPU:1, one launch (start us, length us, event | category | flops | bytes accessed | tf_op | source)
XLA Modules:
  0.0 47.0 jit_solution(13461694531982439957)
XLA Ops:
  0.0 46.3 %shared_prefix.1 = bf16[8,96,128]{2,1,0:T(8,128)(2,1)S(1)} custom-call(s32[1,32]{1,0:T(1,128)} %bitcast.31, s32[1,64]{1,0:T(1,128)} %bitcast.32, s32[1,32]{1,0:T(1,128)} %bitcast.33, bf16[32,3,8,128]{3,2,1,0:T(8,128)(2,1)} %bitcast.25, bf16[768,128]{1,0:T(8,128)(2,1)} %bitcast.26, bf16[512,128]{1,0:T(8,128)(2,1)} %bitcast.27, bf16[512,128]{1,0:T(8,128)(2,1)} %bitcast.28, ...), custom_call_target="tpu_custom_call" | custom-call | flops 1200000000 | bytes 3000000 | tf_op jit(solution)/shard_map/shared_prefix/pallas_call | solution.py:550
  46.3 0.7 %copy.13 = bf16[4,8,8,3,128]{4,2,1,3,0:T(8,128)(2,1)} copy(bf16[4,8,8,3,128]{4,2,3,0,1:T(8,128)(2,1)S(1)} %bitcast.22) | data formatting | bytes 393216 | tf_op jit(solution)/shard_map/transpose | solution.py:625

commit v12 on v9

--- a/solution.py
+++ b/solution.py
@@ -72,6 +72,7 @@
     own_sem,
     above_here,
     below_here,
+    lower_here,
     far_q_send_sem,
     far_q_recv_sem,
     far_o_send_sem,
@@ -101,7 +102,7 @@
         )
 
     above, below = (head + 1) % 8, (head + 7) % 8
-    for peer in (right, left, plane + ahead, plane + behind, plane + sibling):
+    for peer in (left, plane + ahead, plane + behind, plane + sibling):
         greet(peer, head)
     greet(pre, above)
     greet(pre, below)
@@ -198,9 +199,9 @@
             device_id_type=MESH,
         )
 
-    pl.semaphore_wait(barrier, 7)
-    for way in range(2):
-        ring(way, 1, 0).start()
+    pl.semaphore_wait(barrier, 6)
+    ring(0, 1, 0).start()
+    pl.semaphore_signal(lower_here, inc=1, device_id=(right, head), device_id_type=MESH)
     for i in (4, 5, 2, 7, 8, 6, 9, 10):
         loads[i].start()
 
@@ -275,8 +276,9 @@
     )
     index_rows[16:24, :] = slots.astype(jnp.int32)
 
-    for way in range(2):
-        ring(way, 1, 1).start()
+    ring(0, 1, 1).start()
+    pl.semaphore_wait(lower_here, 1)
+    ring(1, 1, 0).start()
 
     loads[4].wait()
     loads[5].wait()
@@ -330,6 +332,7 @@
                 ring(way, hop + 1, which).start()
 
     pairs(0)
+    ring(1, 1, 1).start()
     pairs(4)
     pass_on(1, 0)
     hand_on(0, (5, 7))
@@ -595,6 +598,7 @@
             dma,
             pltpu.SemaphoreType.REGULAR((3,)),
             pltpu.SemaphoreType.REGULAR((2,)),
+            pltpu.SemaphoreType.REGULAR,
             dma((2,)),
             dma((2,)),
             dma,

time: 47.3 us -> 48.5 us (1.025)
  Pallas kernels: 46.4 us -> 47.5 us
    pallas_call x1, Pallas kernels: 46.4 us -> 47.5 us  [shards(): pl.pallas_call(kernel, out_shape=pltpu.VMEM((8, 96, 128), bf16), in_specs...]
where the time goes in v12:
time: 48.5 us; the launch traced here: 48.2 us
  Pallas kernels  47.5 us (98%)
  local copies, waits for them, and re-layouts  0.72 us (1%)
    pallas_call x1, Pallas kernels, shards(): pl.pallas_call(kernel, out_shape=pltpu.VMEM((8, 96, 128), bf16), in_specs...  47.5 us

profile of v12, /device:TPU:1, one launch (start us, length us, event | category | flops | bytes accessed | tf_op | source)
XLA Modules:
  0.0 48.2 jit_solution(7490642158356565840)
XLA Ops:
  0.0 47.5 %shared_prefix.1 = bf16[8,96,128]{2,1,0:T(8,128)(2,1)S(1)} custom-call(s32[1,32]{1,0:T(1,128)} %bitcast.31, s32[1,64]{1,0:T(1,128)} %bitcast.32, s32[1,32]{1,0:T(1,128)} %bitcast.33, bf16[32,3,8,128]{3,2,1,0:T(8,128)(2,1)} %bitcast.25, bf16[768,128]{1,0:T(8,128)(2,1)} %bitcast.26, bf16[512,128]{1,0:T(8,128)(2,1)} %bitcast.27, bf16[512,128]{1,0:T(8,128)(2,1)} %bitcast.28, ...), custom_call_target="tpu_custom_call" | custom-call | flops 1200000000 | bytes 3000000 | tf_op jit(solution)/shard_map/shared_prefix/pallas_call | solution.py:553
  47.5 0.7 %copy.13 = bf16[4,8,8,3,128]{4,2,1,3,0:T(8,128)(2,1)} copy(bf16[4,8,8,3,128]{4,2,3,0,1:T(8,128)(2,1)S(1)} %bitcast.22) | data formatting | bytes 393216 | tf_op jit(solution)/shard_map/transpose | solution.py:629

commit v13 on v9

--- a/solution.py
+++ b/solution.py
@@ -330,8 +330,8 @@
                 ring(way, hop + 1, which).start()
 
     pairs(0)
+    pass_on(1, 0)
     pairs(4)
-    pass_on(1, 0)
     hand_on(0, (5, 7))
     hand_on(1, (8,))
     pairs(8)

time: 47.3 us -> 48.3 us (1.021)
  Pallas kernels: 46.4 us -> 47.3 us
    pallas_call x1, Pallas kernels: 46.4 us -> 47.3 us  [shards(): pl.pallas_call(kernel, out_shape=pltpu.VMEM((8, 96, 128), bf16), in_specs...]
where the time goes in v13:
time: 48.3 us; the launch traced here: 48 us
  Pallas kernels  47.3 us (98%)
  local copies, waits for them, and re-layouts  0.72 us (1%)
    pallas_call x1, Pallas kernels, shards(): pl.pallas_call(kernel, out_shape=pltpu.VMEM((8, 96, 128), bf16), in_specs...  47.3 us

profile of v13, /device:TPU:1, one launch (start us, length us, event | category | flops | bytes accessed | tf_op | source)
XLA Modules:
  0.0 48.0 jit_solution(11257904643237411931)
XLA Ops:
  0.0 47.3 %shared_prefix.1 = bf16[8,96,128]{2,1,0:T(8,128)(2,1)S(1)} custom-call(s32[1,32]{1,0:T(1,128)} %bitcast.31, s32[1,64]{1,0:T(1,128)} %bitcast.32, s32[1,32]{1,0:T(1,128)} %bitcast.33, bf16[32,3,8,128]{3,2,1,0:T(8,128)(2,1)} %bitcast.25, bf16[768,128]{1,0:T(8,128)(2,1)} %bitcast.26, bf16[512,128]{1,0:T(8,128)(2,1)} %bitcast.27, bf16[512,128]{1,0:T(8,128)(2,1)} %bitcast.28, ...), custom_call_target="tpu_custom_call" | custom-call | flops 1200000000 | bytes 3000000 | tf_op jit(solution)/shard_map/shared_prefix/pallas_call | solution.py:550
  47.3 0.7 %copy.13 = bf16[4,8,8,3,128]{4,2,1,3,0:T(8,128)(2,1)} copy(bf16[4,8,8,3,128]{4,2,3,0,1:T(8,128)(2,1)S(1)} %bitcast.22) | data formatting | bytes 393216 | tf_op jit(solution)/shard_map/transpose | solution.py:625
